TPU v7x, 32 devices: a whole 2x2x4 slice. The times are simulated.
32 devices in a mesh: kpool: 2 (over x), fft: 16 (over z, y, core).
Axes of the slice: x: 2, y: 2, z: 4, core: 2. Of those that a mesh axis runs over, the one named last changes fastest.
Arguments:
- orbitals: float32 [2, 8, 4, 4096], P('kpool', None, None, 'fft'), may hold values from -6 to 6
- response: float32 [2, 8, 4, 4096], P('kpool', None, None, 'fft'), may hold values from -6 to 6
- residual: float32 [2, 8, 4, 4096], P('kpool', None, None, 'fft'), may hold values from -9 to 9
- old_direction: float32 [2, 8, 4, 4096], P('kpool', None, None, 'fft'), may hold values from -6 to 6
- old_norm: float32 [2, 8], P('kpool'), may hold values from 2457.6 to 1802240
- band_energy: float32 [2, 8], P('kpool'), may hold values from -1 to 0.4
- kinetic: float32 [2, 4096], P('kpool', 'fft'), may hold values from 0.5 to 20
- form_factor: float32 [2, 2, 16, 4096], P('kpool', None, None, 'fft'), may hold values from -0.09375 to 0.09375
- sphere_index: int32 [2, 4096], P('kpool', 'fft'), may hold values from 0 to 262143, as said below
- atom_positions: float32 [3, 64], replicated, may hold values from 0 to 1
- proj_atom: int32 [1024], replicated, may hold values from 0 to 63
- coupling: float32 [2, 32, 32], replicated, may hold values from -0.03 to 3
- potential: float32 [4, 64, 4096], P(None, 'fft'), may hold values from -0.3 to 2
Outputs:
- response_next: float32 [2, 8, 4, 4096], P('kpool', None, None, 'fft')
- residual_next: float32 [2, 8, 4, 4096], P('kpool', None, None, 'fft')
- direction: float32 [2, 8, 4, 4096], P('kpool', None, None, 'fft')
- induced_density: float32 [4, 64, 4096], P(None, 'fft')
Inputs may be any that keep to these rules, and one draw needn't show every extreme that they name: `sphere_index`: within one point the entries are distinct. Entry j = b * 32 + t (t < 32) has gz = (t - 16) mod 64, and the 32 entries of one b share one column (gx, gy), so the plane waves of every device are whole columns. The columns of one point are the 128 columns nearest the anchor in signed frequencies f(gx)^2 + f(gy)^2, ties broken at random, in a random order.
All inputs are finite; a program needn't handle non-finite values.
Results may differ from a plain program's by a relative error of at most 0.0003.
Values sent between devices are 32-bit elements; how exact they have to be, the bound alone decides.
A program may use at most 128 MiB of HBM per device.

v0:
```python
import functools
import math

import jax
import jax.numpy as jnp
import numpy as np
from jax import lax
from jax.experimental import pallas as pl
from jax.experimental.pallas import tpu as pltpu
from jax.sharding import PartitionSpec as P

NG = 64
STICK_LEN = 32

TWO_PI = 2.0 * math.pi
SMALL_TERM = 1e-06
HIGH = lax.Precision.HIGH


def contract(form_text, *operands):
    return jnp.einsum(form_text, *operands, precision=HIGH)


def line_matrix(columns):
    depth = (np.arange(STICK_LEN) - STICK_LEN // 2) % NG
    angle = 2.0 * np.pi / NG * (np.outer(np.arange(NG), depth) % NG)
    cosine, sine = np.cos(angle), np.sin(angle)
    parts = np.stack([np.stack([cosine, -sine], 1), np.stack([sine, cosine], 1)], 1)
    full = np.einsum("zdct,SR->zdScRt", parts, np.eye(columns))
    return full.reshape(NG * 2 * columns, 2 * columns * STICK_LEN).astype(np.float32)


def signed(values):
    return jnp.where(values < NG // 2, values, values - NG).astype(jnp.float32)


def column_phases(col_x, col_y):
    steps = jnp.arange(2 * NG, dtype=jnp.int32)
    wound = (col_x[:, None] * (steps // NG)[None, :] + col_y[:, None] * (steps % NG)[None, :]) % NG
    turn = jnp.broadcast_to(2 * col_x[:, None] % NG, wound.shape)
    angle = TWO_PI / NG * jnp.stack([wound, turn]).astype(jnp.float32)
    return jnp.stack([jnp.cos(angle), jnp.sin(angle)], 1)


def split(values):
    high = values.astype(jnp.bfloat16)
    return high, (values - high.astype(jnp.float32)).astype(jnp.bfloat16)


def product(left, right, dims):
    def one(a, b):
        return lax.dot_general(a, b, (dims, ((), ())), preferred_element_type=jnp.float32)

    return one(left[0], right[0]) + (one(left[0], right[1]) + one(left[1], right[0]))


def planes_kernel(
    slab, bands, values_ref, phase_ref, potential_ref,
    sticks_ref, curve_ref, base_ref, slope_ref,
    carry, high, low,
):
    count = phase_ref.shape[2]
    tile = potential_ref.shape[2]

    @pl.when(pl.program_id(0) == 0)
    def _():
        carry[...] = phase_ref[0]
        sticks_ref[...] = jnp.zeros_like(sticks_ref)
        curve_ref[...] = jnp.zeros_like(curve_ref)

    for pair in range(tile // (2 * NG)):
        cosine, sine = carry[0], carry[1]
        first, second = pair * 2 * NG, tile + pair * 2 * NG
        cos_parts, sin_parts = split(cosine), split(sine)
        for out, c, s in zip((high, low), cos_parts, sin_parts):
            out[0:count, first : first + 2 * NG] = c
            out[0:count, second : second + 2 * NG] = s
            out[count:, first : first + 2 * NG] = -s
            out[count:, second : second + 2 * NG] = c
        turn_c, turn_s = phase_ref[1, 0], phase_ref[1, 1]
        carry[0] = cosine * turn_c - sine * turn_s
        carry[1] = sine * turn_c + cosine * turn_s

    table = (high[...], low[...])
    grid = product(split(values_ref[...]), table, ((1,), (0,)))
    total = jnp.zeros((bands, tile), jnp.float32)
    fields = []
    for z in range(slab):

        def part(field, spin):
            row = ((z * 3 + field) * 2 + spin) * bands
            block = grid[row : row + bands]
            return block[:, :tile], block[:, tile:]

        (ur, ui), (dr, di) = part(0, 0), part(0, 1)

        def terms(up, down):
            (pr, pi), (qr, qi) = up, down
            same_up = ur * pr + ui * pi
            same_down = dr * qr + di * qi
            return (
                same_up + same_down,
                ur * qr + ui * qi + dr * pr + di * pi,
                ur * qi - ui * qr - (dr * pi - di * pr),
                same_up - same_down,
            )

        (pr, pi), (qr, qi) = part(2, 0), part(2, 1)
        for mu, value in enumerate(terms(part(1, 0), part(1, 1))):
            base_ref[mu, z : z + 1, :] = jnp.sum(value, axis=0, keepdims=True)
        for mu, value in enumerate(terms((pr, pi), (qr, qi))):
            slope_ref[mu, z] = value
        scalar, bx, by, bz = (potential_ref[k, z : z + 1, :] for k in range(4))
        upper, lower = scalar + bz, scalar - bz
        new_pr = upper * pr + bx * qr + by * qi
        new_pi = upper * pi + bx * qi - by * qr
        new_qr = bx * pr - by * pi + lower * qr
        new_qi = bx * pi + by * pr + lower * qi
        total = total + (pr * new_pr + pi * new_pi + qr * new_qr + qi * new_qi)
        fields.append(jnp.concatenate([new_pr, new_pi], axis=1))
        fields.append(jnp.concatenate([new_qr, new_qi], axis=1))
    sticks_ref[...] += product(split(jnp.concatenate(fields, axis=0)), table, ((1,), (1,)))
    curve_ref[...] += total


def planes(values, phases, potential, bands):
    slab, cells = potential.shape[1], potential.shape[2]
    count = phases.shape[2]
    tile = 8 * NG
    return pl.pallas_call(
        functools.partial(planes_kernel, slab, bands),
        grid=(cells // tile,),
        in_specs=[
            pl.BlockSpec(values.shape, lambda i: (0, 0)),
            pl.BlockSpec(phases.shape, lambda i: (0, 0, 0, 0)),
            pl.BlockSpec((4, slab, tile), lambda i: (0, 0, i)),
        ],
        out_specs=[
            pl.BlockSpec((slab * 2 * bands, 2 * count), lambda i: (0, 0)),
            pl.BlockSpec((bands, tile), lambda i: (0, 0)),
            pl.BlockSpec((4, slab, tile), lambda i: (0, 0, i)),
            pl.BlockSpec((4, slab, bands, tile), lambda i: (0, 0, 0, i)),
        ],
        out_shape=[
            jax.ShapeDtypeStruct((slab * 2 * bands, 2 * count), jnp.float32),
            jax.ShapeDtypeStruct((bands, tile), jnp.float32),
            jax.ShapeDtypeStruct((4, slab, cells), jnp.float32),
            jax.ShapeDtypeStruct((4, slab, bands, cells), jnp.float32),
        ],
        scratch_shapes=[
            pltpu.VMEM((2, count, 2 * NG), jnp.float32),
            pltpu.VMEM((2 * count, 2 * tile), jnp.bfloat16),
            pltpu.VMEM((2 * count, 2 * tile), jnp.bfloat16),
        ],
        compiler_params=pltpu.CompilerParams(vmem_limit_bytes=40 * 2**20),
    )(values, phases, potential)


def exchange(values):
    return lax.all_to_all(values, "fft", split_axis=0, concat_axis=0, tiled=True)


def per_device(
    orbitals,
    response,
    residual,
    old_direction,
    old_norm,
    band_energy,
    kinetic,
    form_factor,
    sphere_index,
    atom_positions,
    proj_atom,
    coupling,
    potential,
):
    groups = lax.axis_size("fft")
    pools = lax.axis_size("kpool")
    bands = orbitals.shape[1]
    points = sphere_index.shape[1]
    columns = points // STICK_LEN
    slab = NG // groups
    atoms = atom_positions.shape[1]
    channels = form_factor.shape[2]
    share = atoms // groups
    cells = NG * NG
    scale = 2.0 / (pools * points * groups)
    lines = jnp.asarray(line_matrix(columns))

    own = sphere_index[0].reshape(columns, STICK_LEN)[:, 0] // NG
    res_now = residual[0]
    first = jnp.concatenate(
        [
            jnp.sum(res_now * res_now, axis=(1, 2)),
            (own // NG).astype(jnp.float32),
            (own % NG).astype(jnp.float32),
        ]
    )
    first = exchange(jnp.broadcast_to(first[None], (groups, first.shape[0])))
    norm_now = jnp.sum(first[:, :bands], axis=0)
    col_x = first[:, bands : bands + columns].reshape(-1).astype(jnp.int32)
    col_y = first[:, bands + columns :].reshape(-1).astype(jnp.int32)
    phases = column_phases(col_x, col_y)
    direction = res_now + (norm_now / old_norm[0])[:, None, None] * old_direction[0]

    index = sphere_index[0]
    theta = TWO_PI * (
        atom_positions[0][:, None] * signed(index // cells)[None, :]
        + atom_positions[1][:, None] * signed(index // NG % NG)[None, :]
        + atom_positions[2][:, None] * signed(index % NG)[None, :]
    )
    cosine, sine = jnp.cos(theta)[:, None, :], jnp.sin(theta)[:, None, :]
    real_part, imag_part = form_factor[0, 0][None], form_factor[0, 1][None]
    tabs = jnp.stack(
        [real_part * cosine + imag_part * sine, imag_part * cosine - real_part * sine]
    ).reshape(2 * atoms * channels, points)
    slots = proj_atom.reshape(channels, -1)
    number = jnp.sum(
        (slots[None] == jnp.arange(atoms, dtype=jnp.int32)[:, None, None]).astype(jnp.float32), axis=2
    )

    fields = jnp.concatenate([orbitals, response, direction[None]], 0)
    sent = lax.dot_general(
        lines, fields.reshape(6 * bands, 2 * points), (((1,), (1,)), ((), ())), precision=HIGH
    )
    amps = lax.dot_general(
        tabs, direction.reshape(4 * bands, points), (((1,), (1,)), ((), ())), precision=HIGH
    ).reshape(2, atoms, channels, 2 * bands, 2)
    amps = jnp.stack(
        [amps[0, ..., 0] + amps[1, ..., 1], amps[0, ..., 1] - amps[1, ..., 0]], 1
    )
    chunk = slab * 2 * columns * 6 * bands
    got = exchange(
        jnp.concatenate([sent.reshape(groups, chunk), amps.reshape(groups, -1)], axis=1)
    )
    values = got[:, :chunk].reshape(groups, slab, 2, columns, 3, bands, 2)
    values = jnp.transpose(values, (1, 4, 6, 5, 2, 0, 3)).reshape(slab * 6 * bands, -1)
    sticks, curve, base, slope = planes(values, phases, potential, bands)
    curve = jnp.sum(curve, axis=1) / (NG * cells)

    me = lax.axis_index("fft")
    mine = lax.dynamic_slice_in_dim(number, me * share, share, 0)
    summed = jnp.sum(got[:, chunk:], axis=0).reshape(share, 2, channels, bands, 2)
    summed = summed * mine[:, None, :, None, None]
    herm_real = (0.5 * (coupling[0] + coupling[0].T)).reshape(2, channels, 2, channels)
    herm_imag = (0.5 * (coupling[1] - coupling[1].T)).reshape(2, channels, 2, channels)
    mixing = jnp.stack(
        [jnp.stack([herm_real, -herm_imag], 0), jnp.stack([herm_imag, herm_real], 0)], 0
    )
    mixed = contract("pqscte,aqent->apcns", mixing, summed)
    curve = curve + jnp.sum(mixed * summed, axis=(0, 1, 2, 4))
    local = kinetic[0][None, :] - band_energy[0][:, None]
    curve = curve + jnp.sum(local[:, None, :] * direction * direction, axis=(1, 2))
    mixed = (mixed * mine[:, None, :, None, None]).reshape(1, -1)

    sticks = sticks.reshape(slab, 2, bands, 2, groups, columns)
    sticks = jnp.transpose(sticks, (4, 2, 1, 0, 3, 5)).reshape(groups, -1)
    width = sticks.shape[1]
    shared = jnp.concatenate([mixed, curve[None]], axis=1)
    back = exchange(
        jnp.concatenate([sticks, jnp.broadcast_to(shared, (groups, shared.shape[1]))], axis=1)
    )
    curvature = jnp.sum(back[:, -bands:], axis=0)
    sticks = back[:, :width].reshape(groups, 2 * bands, -1)
    sticks = jnp.transpose(sticks, (1, 0, 2)).reshape(2 * bands, -1)
    potential_term = jnp.dot(sticks, lines, precision=HIGH).reshape(bands, 4, points) / (NG * cells)
    coupled = back[:, width:-bands].reshape(atoms, 2, channels, 2 * bands)
    coupled = jnp.transpose(coupled, (1, 3, 0, 2)).reshape(2, 2 * bands, atoms * channels)
    weights = jnp.stack(
        [
            jnp.stack([coupled[0], -coupled[1]], 1),
            jnp.stack([coupled[1], coupled[0]], 1),
        ],
        1,
    ).reshape(4 * bands, 2 * atoms * channels)
    nonlocal_term = jnp.dot(weights, tabs, precision=HIGH).reshape(bands, 4, points)
    image = local[:, None, :] * direction + potential_term + nonlocal_term
    step = norm_now / (curvature + SMALL_TERM)
    next_response = response[0] + step[:, None, None] * direction
    next_residual = res_now - step[:, None, None] * image
    density = (base + jnp.sum(slope * step[None, None, :, None], axis=2)) * scale
    if pools == 2:
        density = density + lax.ppermute(density, "kpool", [(0, 1), (1, 0)])
    else:
        density = lax.psum(density, "kpool")
    return (next_response[None], next_residual[None], direction[None], density)


def solution(mesh):
    in_specs = (
        P("kpool", None, None, "fft"),
        P("kpool", None, None, "fft"),
        P("kpool", None, None, "fft"),
        P("kpool", None, None, "fft"),
        P("kpool", None),
        P("kpool", None),
        P("kpool", "fft"),
        P("kpool", None, None, "fft"),
        P("kpool", "fft"),
        P(),
        P(),
        P(),
        P(None, "fft", None),
    )
    out_specs = (
        P("kpool", None, None, "fft"),
        P("kpool", None, None, "fft"),
        P("kpool", None, None, "fft"),
        P(None, "fft", None),
    )
    return jax.shard_map(
        per_device, mesh=mesh, in_specs=in_specs, out_specs=out_specs, check_vma=False
    )
```

profile of v0, /device:TPU:0, one launch (start us, length us, event | category | flops | bytes accessed | tf_op | source)
XLA Modules:
  0.0 96.3 jit_solution(17928847332123949277)
XLA Ops:
  0.7 0.9 fusion.22
  2.1 1.3 %fusion.27 = (f32[1,256]{1,0:T(1,128)S(1)}, s32[256]{0:T(256)S(1)}, f32[1,256]{1,0:T(1,128)S(1)}, s32[1,256]{1,0:T(1,128)S(1)}) fusion(s32[1,256]{1,0:T(1,128)} %param.22, s32[]{:T(128)} %broadcast.585), kind=kLoop, calls=%fused_computation.106 | loop fusion | flops 11264 | bytes 5124 | tf_op jit(solution)/shard_map/convert_element_type | solution.py:34
  4.4 7.4 %all-to-all-start = ((f32[16,1,24]{2,1,0:T(1,128)}), f32[16,1,24]{2,1,0:T(1,128)S(1)}, u32[]{:S(2)}, u32[]{:S(2)}) async-start(f32[16,1,24]{2,1,0:T(1,128)} %broadcast_in_dim.8), calls=%async_computation | async-start | bytes 16384 | tf_op jit(solution)/shard_map/all_to_all | solution.py:160
  11.8 0.8 slice_bitcast_fusion.7
  12.6 0.8 eq.26
  13.5 0.7 slice_bitcast_fusion.4
  14.3 0.7 slice_bitcast_fusion.2
  15.2 0.8 fusion.25
  16.1 0.8 broadcast_subtract_fusion
  18.3 1.0 %fusion = f32[2,64,16,16,2]{3,2,4,1,0:T(8,128)S(1)} fusion(f32[16,2,256,1,1]{2,1,0,4,3:T(2,128)S(1)} %bitcast.159, f32[1,64,16,256]{3,2,1,0:T(8,128)S(1)} %get-tuple-element.27, f32[1,64,16,256]{3,2,1,0:T(8,128)S(1)} %get-tuple-element.26), kind=kOutput, calls=%fused_computation.1 | convolution fusion | flops 101187584 | bytes 2392064 | tf_op jit(solution)/shard_map/dot_general | solution.py:227
  20.2 2.6 %fusion.35 = f32[1024,48]{1,0:T(8,128)S(1)} fusion(f32[1024,512]{1,0:T(8,128)} %constant.139.clone, f32[48,512]{1,0:T(8,128)S(1)} %reshape.648), kind=kOutput, calls=%fused_computation.128 | convolution fusion | flops 150994944 | bytes 2392064 | tf_op jit(solution)/shard_map/dot_general | solution.py:224
  23.9 1.1 %copy.138 = f32[16,1,5120]{2,1,0:T(1,128)} copy(f32[16,1,5120]{2,0,1:T(8,128)S(1)} %maximum_bitcast_fusion) | data formatting | bytes 655360 | tf_op jit(solution)/shard_map/all_to_all | solution.py:160
  25.0 5.5 %all-to-all-start.1 = ((f32[16,1,5120]{2,1,0:T(1,128)}), f32[16,1,5120]{2,1,0:T(1,128)S(1)}, u32[]{:S(2)}, u32[]{:S(2)}) async-start(f32[16,1,5120]{2,1,0:T(1,128)} %copy.138), calls=%async_computation.1 | async-start | bytes 655360 | tf_op jit(solution)/shard_map/all_to_all | solution.py:160
  31.6 10.1 %all-to-all-done.1 = f32[16,1,5120]{2,1,0:T(1,128)S(1)} async-done(((f32[16,1,5120]{2,1,0:T(1,128)}), f32[16,1,5120]{2,1,0:T(1,128)S(1)}, u32[]{:S(2)}, u32[]{:S(2)}) %all-to-all-start.1) | async-done | bytes 327712 | tf_op jit(solution)/shard_map/all_to_all | solution.py:160
  41.6 2.0 %copy.139 = f32[16,1,5120]{0,2,1:T(8,128)} copy(f32[16,1,5120]{2,1,0:T(1,128)S(1)} %all-to-all-done.1) | data formatting | bytes 655360 | tf_op jit(solution)/shard_map/all_to_all | solution.py:160
  43.6 1.6 %slice_reduce_fusion = f32[2048]{0:T(1024)S(1)} fusion(f32[16,5120]{0,1:T(8,128)} %bitcast.146), kind=kLoop, calls=%fused_computation.10 | loop fusion | flops 30720 | bytes 139264 | tf_op jit(solution)/shard_map/reduce_sum | solution.py:244
  45.1 1.5 %slice.99 = f32[16,3072]{0,1:T(8,128)S(1)} slice(f32[16,5120]{0,1:T(8,128)} %bitcast.147), slice={[0:16], [0:3072]} | slice | bytes 393216 | tf_op jit(solution)/shard_map/slice | solution.py:237
  48.9 2.8 %copy.140 = f32[4,3,2,8,2,16,8]{6,5,4,3,2,1,0:T(8,128)} copy(f32[4,3,2,8,2,16,8]{5,2,3,1,6,4,0:T(2,128)S(1)} %bitcast.149) | data formatting | bytes 393216 | tf_op jit(solution)/shard_map/transpose | solution.py:238
  51.7 3.4 %reshape.652.values_ref = f32[192,256]{1,0:T(8,128)S(1)} reshape(f32[4,3,2,8,2,16,8]{6,5,4,3,2,1,0:T(8,128)} %copy.140) | data formatting | bytes 393216 | tf_op jit(solution)/shard_map/reshape | solution.py:238
  55.1 10.5 %shard_map.165 = (f32[64,256]{1,0:T(8,128)S(1)}, f32[8,512]{1,0:T(8,128)S(1)}, f32[4,4,4096]{2,1,0:T(4,128)S(1)}, f32[4,4,8,4096]{3,2,1,0:T(8,128)S(1)}) custom-call(f32[192,256]{1,0:T(8,128)S(1)} %reshape.652.values_ref, f32[2,2,128,128]{3,2,1,0:T(8,128)S(1)} %pad_maximum_fusion.2.phase_ref, f32[4,4,4096]{2,1,0:T(4,128)S(1)} %copy-done), custom_call_target="tpu_custom_call" | custom-call | tf_op jit(solution)/shard_map/pallas_call | solution.py:130
  65.6 1.6 %reshape.653 = f32[4,2,8,2,16,8]{5,4,3,2,1,0:T(8,128)} reshape(f32[64,256]{1,0:T(8,128)S(1)} %get-tuple-element.8) | data formatting | bytes 131072 | tf_op jit(solution)/shard_map/reshape | solution.py:257
  67.1 1.5 %copy.141 = f32[16,8,2,4,2,8]{0,5,4,3,2,1:T(8,128)S(1)} copy(f32[16,8,2,4,2,8]{5,0,4,1,2,3:T(8,128)} %bitcast.151) | data formatting | bytes 131072 | tf_op jit(solution)/shard_map/transpose | solution.py:258
  69.1 0.8 all_to_all.27
  69.9 3.5 %all-to-all-start.2 = ((f32[16,1,3080]{2,1,0:T(1,128)}), f32[16,1,3080]{2,1,0:T(1,128)S(1)}, u32[]{:S(2)}, u32[]{:S(2)}) async-start(f32[16,1,3080]{2,1,0:T(1,128)} %all_to_all.27), calls=%async_computation.2 | async-start | bytes 409600 | tf_op jit(solution)/shard_map/all_to_all | solution.py:160
  73.4 3.0 %pad_maximum_fusion = f32[2,64,16,256]{3,2,1,0:T(8,128)} fusion(f32[1,64,16,256]{3,2,1,0:T(8,128)} %copy-done.2, f32[1,64,16,256]{3,2,1,0:T(8,128)} %copy-done.1), kind=kLoop, calls=%fused_computation | loop fusion | flops 524288 | bytes 4194304 | tf_op jit(solution)/shard_map/stack | solution.py:215
  76.5 6.0 %all-to-all-done.2 = f32[16,1,3080]{2,1,0:T(1,128)S(1)} async-done(((f32[16,1,3080]{2,1,0:T(1,128)}), f32[16,1,3080]{2,1,0:T(1,128)S(1)}, u32[]{:S(2)}, u32[]{:S(2)}) %all-to-all-start.2) | async-done | bytes 197152 | tf_op jit(solution)/shard_map/all_to_all | solution.py:160
  82.8 2.2 %convolution_multiply_fusion = f32[16,512]{1,0:T(8,128)S(1)} fusion(f32[16,1024]{1,0:T(8,128)S(1)} %reshape.659, f32[1024,512]{1,0:T(8,128)} %constant.139.clone), kind=kOutput, calls=%fused_computation.5 | convolution fusion | flops 50339840 | bytes 2195456 | tf_op jit(solution)/shard_map/dot_general | solution.py:267
  85.7 0.7 multiply_reduce_fusion
  86.5 1.6 %collective-permute-start = (f32[4,4,4096]{2,1,0:T(4,128)S(1)}, f32[4,4,4096]{2,1,0:T(4,128)}, u32[]{:S(2)}, u32[]{:S(2)}) collective-permute-start(f32[4,4,4096]{2,1,0:T(4,128)S(1)} %add_multiply_fusion), channel_id=1, source_target_pairs={{0,16},{16,0},{1,17},{17,1},{2,18},{18,2},{3,19},{19,3},{4,20},{20... | collective-permute-start | bytes 786440 | tf_op jit(solution)/shard_map/ppermute | solution.py:284
  90.1 1.4 %fusion.4 = f32[1,8,4,256]{3,2,1,0:T(4,128)} fusion(f32[8,4,2048]{2,1,0:T(4,128)S(1)} %dot_general.24, f32[2048,256,1]{1,0,2:T(8,128)S(1)} %bitcast.148, f32[8,4,256]{2,1,0:T(4,128)S(1)} %copy-done.8, f32[1,8,4,256]{3,2,1,0:T(4,128)S(1)} %copy-done.4, f32[1,8,4,256]{3,2,1,0:T(4,128)S(1)} %copy-done.7, f32[8]{0:T(128)S(1)} %add_divide_fusion, ...), kind=kOutput, calls=%fused_computation.9 | convolution fusion | flops 100720640 | bytes 2498624 | tf_op jit(solution)/shard_map/dot_general | solution.py:277
  92.1 2.4 %collective-permute-done = f32[4,4,4096]{2,1,0:T(4,128)} collective-permute-done((f32[4,4,4096]{2,1,0:T(4,128)S(1)}, f32[4,4,4096]{2,1,0:T(4,128)}, u32[]{:S(2)}, u32[]{:S(2)}) %collective-permute-start) | collective-permute-done | bytes 262176 | tf_op jit(solution)/shard_map/ppermute | solution.py:284
  94.6 1.7 %add.227 = f32[4,4,4096]{2,1,0:T(4,128)} add(f32[4,4,4096]{2,1,0:T(4,128)S(1)} %add_multiply_fusion, f32[4,4,4096]{2,1,0:T(4,128)} %collective-permute-done) | non-fusion elementwise | flops 65536 | bytes 786432 | tf_op jit(solution)/shard_map/add | solution.py:284
  (99 shorter events, 12.5 us)
Async XLA Ops:
  0.6 17.5 %copy-start.4 = (f32[1,8,4,256]{3,2,1,0:T(4,128)S(1)}, f32[1,8,4,256]{3,2,1,0:T(4,128)}, u32[]{:S(2)}) copy-start(f32[1,8,4,256]{3,2,1,0:T(4,128)} %param.16) | copy-start | bytes 98308
  0.6 17.5 %copy-start.12 = (f32[1,8]{1,0:T(1,128)S(1)}, f32[1,8]{1,0:T(1,128)}, u32[]{:S(2)}) copy-start(f32[1,8]{1,0:T(1,128)} %param.18) | copy-start | bytes 100
  0.7 17.5 %copy-start.6 = (f32[1,8,4,256]{3,2,1,0:T(4,128)S(1)}, f32[1,8,4,256]{3,2,1,0:T(4,128)}, u32[]{:S(2)}) copy-start(f32[1,8,4,256]{3,2,1,0:T(4,128)} %param.17) | copy-start | bytes 98308
  4.4 13.7 %all-to-all-start = ((f32[16,1,24]{2,1,0:T(1,128)}), f32[16,1,24]{2,1,0:T(1,128)S(1)}, u32[]{:S(2)}, u32[]{:S(2)}) async-start(f32[16,1,24]{2,1,0:T(1,128)} %broadcast_in_dim.8), calls=%async_computation | async-start | bytes 16384 | tf_op jit(solution)/shard_map/all_to_all | solution.py:160
  17.6 1.8 %copy-start.1 = (f32[1,64,16,256]{3,2,1,0:T(8,128)}, f32[1,64,16,256]{3,2,1,0:T(8,128)S(1)}, u32[]{:S(2)}) copy-start(f32[1,64,16,256]{3,2,1,0:T(8,128)S(1)} %get-tuple-element.26) | copy-start | bytes 3145732
  17.6 1.8 %copy-start.2 = (f32[1,64,16,256]{3,2,1,0:T(8,128)}, f32[1,64,16,256]{3,2,1,0:T(8,128)S(1)}, u32[]{:S(2)}) copy-start(f32[1,64,16,256]{3,2,1,0:T(8,128)S(1)} %get-tuple-element.27) | copy-start | bytes 3145732
  18.3 73.2 %copy-start.5 = (f32[1,8,4,256]{3,2,1,0:T(4,128)}, f32[1,8,4,256]{3,2,1,0:T(4,128)S(1)}, u32[]{:S(2)}) copy-start(f32[1,8,4,256]{3,2,1,0:T(4,128)S(1)} %multiply_add_fusion.3) | copy-start | bytes 98308
  19.4 0.8 copy-start.9
  19.4 0.8 copy-start.11
  25.0 16.6 %all-to-all-start.1 = ((f32[16,1,5120]{2,1,0:T(1,128)}), f32[16,1,5120]{2,1,0:T(1,128)S(1)}, u32[]{:S(2)}, u32[]{:S(2)}) async-start(f32[16,1,5120]{2,1,0:T(1,128)} %copy.138), calls=%async_computation.1 | async-start | bytes 655360 | tf_op jit(solution)/shard_map/all_to_all | solution.py:160
  51.7 3.4 %copy-start = (f32[4,4,4096]{2,1,0:T(4,128)S(1)}, f32[4,4,4096]{2,1,0:T(4,128)}, u32[]{:S(2)}) copy-start(f32[4,4,4096]{2,1,0:T(4,128)} %potential_ref.1) | copy-start | bytes 786436
  69.9 12.6 %all-to-all-start.2 = ((f32[16,1,3080]{2,1,0:T(1,128)}), f32[16,1,3080]{2,1,0:T(1,128)S(1)}, u32[]{:S(2)}, u32[]{:S(2)}) async-start(f32[16,1,3080]{2,1,0:T(1,128)} %all_to_all.27), calls=%async_computation.2 | async-start | bytes 409600 | tf_op jit(solution)/shard_map/all_to_all | solution.py:160
  86.5 8.1 %collective-permute-start = (f32[4,4,4096]{2,1,0:T(4,128)S(1)}, f32[4,4,4096]{2,1,0:T(4,128)}, u32[]{:S(2)}, u32[]{:S(2)}) collective-permute-start(f32[4,4,4096]{2,1,0:T(4,128)S(1)} %add_multiply_fusion), channel_id=1, source_target_pairs={{0,16},{16,0},{1,17},{17,1},{2,18},{18,2},{3,19},{19,3},{4,20},{20... | collective-permute-start | bytes 786440 | tf_op jit(solution)/shard_map/ppermute | solution.py:284
  88.5 1.6 %copy-start.3 = (f32[2,64,16,256]{3,2,1,0:T(8,128)S(1)}, f32[2,64,16,256]{3,2,1,0:T(8,128)}, u32[]{:S(2)}) copy-start(f32[2,64,16,256]{3,2,1,0:T(8,128)} %pad_maximum_fusion) | copy-start | bytes 6291460
  88.7 1.4 %copy-start.7 = (f32[1,8,4,256]{3,2,1,0:T(4,128)S(1)}, f32[1,8,4,256]{3,2,1,0:T(4,128)}, u32[]{:S(2)}) copy-start(f32[1,8,4,256]{3,2,1,0:T(4,128)} %param.17) | copy-start | bytes 98308
  88.7 1.4 %copy-start.8 = (f32[8,4,256]{2,1,0:T(4,128)S(1)}, f32[8,4,256]{2,1,0:T(4,128)}, u32[]{:S(2)}) copy-start(f32[8,4,256]{2,1,0:T(4,128)} %div.101) | copy-start | bytes 98308
  88.9 2.6 %copy-start.10 = (f32[1,8,4,256]{3,2,1,0:T(4,128)S(1)}, f32[1,8,4,256]{3,2,1,0:T(4,128)}, u32[]{:S(2)}) copy-start(f32[1,8,4,256]{3,2,1,0:T(4,128)} %param.15) | copy-start | bytes 98308
where the time goes:
time: 97.3 us; the launch traced here: 96.3 us
  local copies, waits for them, and re-layouts  25.9 us (27%)
  waiting for transfers between devices  19 us (20%)
  starting transfers between devices  18 us (18%)
  other arithmetic  14.1 us (14%)
  Pallas kernels  10.5 us (11%)
  matrix products  7.67 us (8%)
  between operations  1.14 us (1%)
    all_to_all x3, waiting for transfers between devices, exchange(): lax.all_to_all(values, 'fft', split_axis=0, concat_axis=0, tiled=True)  16.6 us
    all_to_all x3, starting transfers between devices, exchange(): lax.all_to_all(values, 'fft', split_axis=0, concat_axis=0, tiled=True)  16.4 us
    pallas_call x1, Pallas kernels, planes(): pl.pallas_call(functools.partial(planes_kernel, slab, bands), grid=(cells...  10.5 us
    all_to_all x3, local copies, waits for them, and re-layouts, exchange(): lax.all_to_all(values, 'fft', split_axis=0, concat_axis=0, tiled=True)  3.82 us
    reshape x1, local copies, waits for them, and re-layouts, per_device(): jnp.transpose(values, (1, 4, 6, 5, 2, 0, 3)).reshape(slab * 6 * bands, -1)  3.39 us
    another operation x1, other arithmetic, per_device(): jnp.stack([real_part * cosine + imag_part * sine, imag_part * cosine - re...  3.04 us
    transpose x1, local copies, waits for them, and re-layouts, per_device(): jnp.transpose(values, (1, 4, 6, 5, 2, 0, 3)).reshape(slab * 6 * bands, -1)  2.78 us
    dot_general x1, matrix products, per_device(): lax.dot_general(lines, fields.reshape(6 * bands, 2 * points), (((1,), (1,...  2.56 us
  transfers between devices with their start and end apart: 4, of which 4 were waited for; matrix products, arithmetic and copies ran while one was open for 14% of the time, Pallas kernels for 0%

commit v1 on v0

v1 whole, which is shorter than its diff:
```python
import functools
import math

import jax
import jax.numpy as jnp
import numpy as np
from jax import lax
from jax.experimental import pallas as pl
from jax.experimental.pallas import tpu as pltpu
from jax.sharding import PartitionSpec as P

NG = 64
STICK_LEN = 32

TWO_PI = 2.0 * math.pi
SMALL_TERM = 1e-06
LANES = 128
FIRST, ENDS, LINES, AMPS, BACK, SHARE = range(6)


def line_matrix(columns, groups):
    slab = NG // groups
    depth = (np.arange(STICK_LEN) - STICK_LEN // 2) % NG
    angle = 2.0 * np.pi / NG * (np.outer(np.arange(NG), depth) % NG)
    cosine, sine = np.cos(angle), np.sin(angle)
    parts = np.stack([np.stack([cosine, -sine], 1), np.stack([sine, cosine], 1)], 1)
    parts = parts.reshape(groups, slab, 2, 2, STICK_LEN)
    full = np.einsum("gzdct,SR->dzgScRt", parts, np.eye(columns))
    full = full.reshape(NG * 2 * columns, 2 * columns * STICK_LEN).astype(np.float32)
    high = full.astype(jnp.bfloat16)
    low = (full - high.astype(np.float32)).astype(jnp.bfloat16)
    return high, low


def signed(values):
    return jnp.where(values < NG // 2, values, values - NG).astype(jnp.float32)


def split(values):
    high = values.astype(jnp.bfloat16)
    return high, (values - high.astype(jnp.float32)).astype(jnp.bfloat16)


def product(left, right, dims):
    def one(a, b):
        return lax.dot_general(a, b, (dims, ((), ())), preferred_element_type=jnp.float32)

    return one(left[0], right[0]) + (one(left[0], right[1]) + one(left[1], right[0]))


def widen(blocks):
    total = sum(block.shape[1] for block in blocks)
    if total < LANES:
        blocks = blocks + [jnp.zeros((blocks[0].shape[0], LANES - total), jnp.float32)]
    return jnp.concatenate(blocks, axis=1)


def step_kernel(
    groups, pools, scale,
    orbitals_ref, response_ref, residual_ref, previous_ref, bands_ref, kinetic_ref, form_ref,
    wound_ref, cosine_ref, sine_ref, number_ref, mixing_ref, potential_ref, line_high, line_low,
    next_response_ref, next_residual_ref, direction_ref, density_ref,
    first_out, first_in, ends_out, ends_in, lines_out, lines_in, amps_out, amps_in,
    back_out, back_in, share_out, share_in, send_sems, recv_sems,
    tab_high, tab_low, carry, turn, high, low, values_high, values_low,
    sticks, curve, slope, pair_out, pair_in, pair_send, pair_recv,
):
    me = lax.axis_index("fft")
    bands = orbitals_ref.shape[0]
    points = orbitals_ref.shape[2]
    columns = points // STICK_LEN
    slab = NG // groups
    cells = NG * NG
    channels = form_ref.shape[1]
    atoms = cosine_ref.shape[0]
    share = atoms // groups
    count = groups * columns
    block = 2 * bands
    tile = high.shape[1] // 2
    steps = cells // tile

    def peer(k):
        return lax.rem(me + k, groups)

    def copy(stage, source, target, other):
        return pltpu.make_async_remote_copy(
            src_ref=source,
            dst_ref=target.at[me],
            send_sem=send_sems.at[stage, other],
            recv_sem=recv_sems.at[stage, me],
            device_id={"fft": other},
            device_id_type=pl.DeviceIdType.MESH,
        )

    def each_peer(action):
        def run(k, _):
            action(peer(k))
            return 0

        lax.fori_loop(1, groups, run, 0)

    def send(stage, out, target, own=False):
        each_peer(lambda other: copy(stage, out if own else out.at[other], target, other).start())
        target[me] = out[...] if own else out[me]

    def arrive(stage, target):
        def action(other):
            pltpu.make_async_remote_copy(
                src_ref=target.at[other],
                dst_ref=target.at[other],
                send_sem=send_sems.at[stage, other],
                recv_sem=recv_sems.at[stage, other],
                device_id={"fft": other},
                device_id_type=pl.DeviceIdType.MESH,
            ).wait_recv()

        each_peer(action)

    barrier = pltpu.get_barrier_semaphore()
    each_peer(
        lambda other: pl.semaphore_signal(
            barrier, inc=1, device_id={"fft": other}, device_id_type=pl.DeviceIdType.MESH
        )
    )
    if pools == 2:
        partner = {"kpool": 1 - lax.axis_index("kpool")}
        pl.semaphore_signal(
            barrier, inc=1, device_id=partner, device_id_type=pl.DeviceIdType.MESH
        )

    norm = jnp.zeros((bands, points), jnp.float32)
    for part in range(4):
        norm = norm + residual_ref[:, part, :] * residual_ref[:, part, :]
    norm = jnp.sum(norm, axis=1, keepdims=True)
    first_out[0] = jnp.broadcast_to(norm, (bands, LANES))
    first_out[1] = wound_ref[...]
    pl.semaphore_wait(barrier, groups - 1 + (1 if pools == 2 else 0))
    send(FIRST, first_out, first_in, own=True)

    lines = (line_high[...], line_low[...])

    def to_lines(rows):
        made = product(lines, split(jnp.concatenate(rows, axis=0)), ((1,), (1,)))
        out = []
        for field in range(len(rows) // 2):
            cuts = [
                made[k * count : (k + 1) * count, field * block : (field + 1) * block]
                for k in range(2 * slab)
            ]
            out.append(widen(cuts).reshape(groups, columns, LANES))
        return out

    def spin_rows(parts):
        return [jnp.concatenate(parts[0:2], axis=1), jnp.concatenate(parts[2:4], axis=1)]

    made = to_lines(
        spin_rows([orbitals_ref[:, part, :] for part in range(4)])
        + spin_rows([response_ref[:, part, :] for part in range(4)])
    )
    ends_out[:, 0] = made[0]
    ends_out[:, 1] = made[1]
    send(ENDS, ends_out, ends_in)

    def fill(group, _):
        for inner in range(share):
            atom = group * share + inner
            c = cosine_ref[pl.ds(atom, 1), :]
            s = sine_ref[pl.ds(atom, 1), :]
            real = split(form_ref[0] * c + form_ref[1] * s)
            imag = split(form_ref[1] * c - form_ref[0] * s)
            row = pl.ds(pl.multiple_of((inner * groups + group) * channels, channels), channels)
            for out, re, im in zip((tab_high, tab_low), real, imag):
                out[row, 0:points] = re
                out[row, points:] = im
        return 0

    lax.fori_loop(0, groups, fill, 0)

    arrive(FIRST, first_in)
    norm = jnp.sum(first_in[:, 0], axis=0)[:, 0:1]
    ratio = norm / bands_ref[0, :, 0:1]
    direction = []
    for part in range(4):
        value = residual_ref[:, part, :] + ratio * previous_ref[:, part, :]
        direction_ref[:, part, :] = value
        direction.append(value)
    lines_out[...] = to_lines(spin_rows(direction))[0]
    send(LINES, lines_out, lines_in)

    plain = jnp.concatenate([direction[0], direction[2], direction[1], direction[3]], axis=0)
    crossed = jnp.concatenate([direction[1], direction[3], -direction[0], -direction[2]], axis=0)
    amps = product(
        (tab_high[...], tab_low[...]),
        split(jnp.concatenate([plain, crossed], axis=1)),
        ((1,), (1,)),
    )
    rows = groups * channels
    amps = widen([amps[k * rows : (k + 1) * rows] for k in range(share)])
    amps_out[...] = amps.reshape(groups, channels, LANES)
    send(AMPS, amps_out, amps_in)

    wound = first_in[:, 1].reshape(count, LANES)
    ahead = jnp.broadcast_to(2.0 * (wound[:, NG : NG + 1] - wound[:, 0:1]), wound.shape)
    carry[0] = jnp.cos(TWO_PI / NG * wound)
    carry[1] = jnp.sin(TWO_PI / NG * wound)
    turn[0] = jnp.cos(TWO_PI / NG * ahead)
    turn[1] = jnp.sin(TWO_PI / NG * ahead)
    local = kinetic_ref[...] - bands_ref[1, :, 0:1]
    own_curve = jnp.zeros((bands, points), jnp.float32)
    for value in direction:
        own_curve = own_curve + local * value * value
    own_curve = jnp.sum(own_curve, axis=1, keepdims=True)
    sticks[...] = jnp.zeros_like(sticks)
    curve[...] = jnp.zeros_like(curve)

    arrive(ENDS, ends_in)
    arrive(LINES, lines_in)
    height = slab * block
    for field in range(3):
        got = lines_in[...] if field == 2 else ends_in[:, field]
        got = got.reshape(count, LANES).T
        got = jnp.concatenate([got[0:height], got[height : 2 * height]], axis=1)
        parts = split(got)
        values_high[field * height : (field + 1) * height] = parts[0]
        values_low[field * height : (field + 1) * height] = parts[1]

    def plane_step(index, _):
        place = pl.ds(pl.multiple_of(index * tile, tile), tile)
        for pair in range(tile // LANES):
            cosine, sine = carry[0], carry[1]
            left, right = pair * LANES, tile + pair * LANES
            for out, c, s in zip((high, low), split(cosine), split(sine)):
                out[0:count, left : left + LANES] = c
                out[0:count, right : right + LANES] = s
                out[count:, left : left + LANES] = -s
                out[count:, right : right + LANES] = c
            carry[0] = cosine * turn[0] - sine * turn[1]
            carry[1] = sine * turn[0] + cosine * turn[1]

        table = (high[...], low[...])
        grid = product((values_high[...], values_low[...]), table, ((1,), (0,)))
        total = curve[...]
        fields = []
        for z in range(slab):

            def part(field, spin):
                row = ((field * slab + z) * 2 + spin) * bands
                cut = grid[row : row + bands]
                return cut[:, :tile], cut[:, tile:]

            (ur, ui), (dr, di) = part(0, 0), part(0, 1)

            def terms(up, down):
                (pr, pi), (qr, qi) = up, down
                same_up = ur * pr + ui * pi
                same_down = dr * qr + di * qi
                return (
                    same_up + same_down,
                    ur * qr + ui * qi + dr * pr + di * pi,
                    ur * qi - ui * qr - (dr * pi - di * pr),
                    same_up - same_down,
                )

            (pr, pi), (qr, qi) = part(2, 0), part(2, 1)
            for mu, value in enumerate(terms(part(1, 0), part(1, 1))):
                row = mu * slab + z
                pair_out[row : row + 1, place] = jnp.sum(value, axis=0, keepdims=True)
            for mu, value in enumerate(terms((pr, pi), (qr, qi))):
                slope[mu * slab + z, :, place] = value
            scalar, bx, by, bz = (potential_ref[k, z : z + 1, place] for k in range(4))
            upper, lower = scalar + bz, scalar - bz
            new_pr = upper * pr + bx * qr + by * qi
            new_pi = upper * pi + bx * qi - by * qr
            new_qr = bx * pr - by * pi + lower * qr
            new_qi = bx * pi + by * pr + lower * qi
            total = total + (pr * new_pr + pi * new_pi + qr * new_qr + qi * new_qi)
            fields.append(jnp.concatenate([new_pr, new_pi], axis=1))
            fields.append(jnp.concatenate([new_qr, new_qi], axis=1))
        curve[...] = total
        sticks[...] += product(table, split(jnp.concatenate(fields, axis=0)), ((1,), (1,)))
        return 0

    lax.fori_loop(0, steps // 2, plane_step, 0)

    arrive(AMPS, amps_in)
    summed = jnp.sum(amps_in[...], axis=0) * number_ref[...]
    mixed_all = product(split(mixing_ref[...]), split(summed), ((1,), (0,)))
    spot = lax.broadcasted_iota(jnp.int32, (channels, LANES), 1) // bands % 4
    mixed = jnp.zeros((channels, LANES), jnp.float32)
    for v in range(4):
        for u in range(4):
            row = (v * 4 + u) * channels
            moved = mixed_all[row : row + channels]
            if u != v:
                moved = pltpu.roll(moved, bands * (u - v) % LANES, 1)
            mixed = mixed + jnp.where(spot == u, moved, 0.0)
    share_out[0:channels] = mixed * number_ref[...]
    pairing = jnp.broadcast_to(jnp.sum(mixed * summed, axis=0, keepdims=True), (bands, LANES))
    lane = lax.broadcasted_iota(jnp.int32, (bands, LANES), 1) % bands
    row = lax.broadcasted_iota(jnp.int32, (bands, LANES), 0)
    own_curve = own_curve + jnp.sum(jnp.where(lane == row, pairing, 0.0), axis=1, keepdims=True)
    send(SHARE, share_out, share_in, own=True)

    lax.fori_loop(steps // 2, steps, plane_step, 0)

    own_curve = own_curve + jnp.sum(curve[...], axis=1, keepdims=True) / (NG * cells)
    made = widen([sticks[0:count], sticks[count:]])
    back_out[:, 0] = made.reshape(groups, columns, LANES)
    back_out[:, 1] = jnp.broadcast_to(
        jnp.broadcast_to(own_curve, (bands, LANES))[None], (groups, bands, LANES)
    )
    send(BACK, back_out, back_in)

    arrive(SHARE, share_in)
    coupled = share_in[...].reshape(groups * channels, LANES).T
    coupled = jnp.concatenate(
        [coupled[k * 2 * block : (k + 1) * 2 * block] for k in range(share)], axis=1
    )
    with_tabs = product(split(coupled), (tab_high[...], tab_low[...]), ((1,), (0,)))
    added_real = with_tabs[0:block, 0:points] - with_tabs[block:, points:]
    added_imag = with_tabs[block:, 0:points] + with_tabs[0:block, points:]
    arrive(BACK, back_in)
    curvature = jnp.sum(back_in[:, 1], axis=0)[:, 0:1]
    step = norm / (curvature + SMALL_TERM)

    for half in range(2):
        for row in range(half * 2 * slab, (half + 1) * 2 * slab):
            moved = jnp.sum(slope[row] * step, axis=0, keepdims=True)
            pair_out[row : row + 1, :] = (pair_out[row : row + 1, :] + moved) * scale
        if pools == 2:
            part = pl.ds(half * 2 * slab, 2 * slab)
            pltpu.make_async_remote_copy(
                src_ref=pair_out.at[part],
                dst_ref=pair_in.at[part],
                send_sem=pair_send.at[half],
                recv_sem=pair_recv.at[half],
                device_id=partner,
                device_id_type=pl.DeviceIdType.MESH,
            ).start()

    got = back_in[:, 0].reshape(count, LANES).T
    got = jnp.concatenate([got[k * block : (k + 1) * block] for k in range(2 * slab)], axis=1)
    term = product(split(got), lines, ((1,), (0,))) / (NG * cells)
    for part in range(4):
        spin = part // 2
        added = (added_real, added_imag)[part % 2][spin * bands : (spin + 1) * bands]
        placed = term[spin * bands : (spin + 1) * bands, part % 2 * points : (part % 2 + 1) * points]
        value = direction_ref[:, part, :]
        image = local * value + placed + added
        next_response_ref[:, part, :] = response_ref[:, part, :] + step * value
        next_residual_ref[:, part, :] = residual_ref[:, part, :] - step * image

    for half in range(2):
        if pools == 2:
            part = pl.ds(half * 2 * slab, 2 * slab)
            pltpu.make_async_remote_copy(
                src_ref=pair_out.at[part],
                dst_ref=pair_in.at[part],
                send_sem=pair_send.at[half],
                recv_sem=pair_recv.at[half],
                device_id=partner,
                device_id_type=pl.DeviceIdType.MESH,
            ).wait()
        for mu in range(2 * half, 2 * half + 2):
            value = pair_out[mu * slab : (mu + 1) * slab]
            if pools == 2:
                value = value + pair_in[mu * slab : (mu + 1) * slab]
            density_ref[mu] = value

    def sent(other):
        copy(FIRST, first_out, first_in, other).wait_send()
        copy(ENDS, ends_out.at[other], ends_in, other).wait_send()
        copy(LINES, lines_out.at[other], lines_in, other).wait_send()
        copy(AMPS, amps_out.at[other], amps_in, other).wait_send()
        copy(BACK, back_out.at[other], back_in, other).wait_send()
        copy(SHARE, share_out, share_in, other).wait_send()

    each_peer(sent)


def per_device(
    orbitals,
    response,
    residual,
    old_direction,
    old_norm,
    band_energy,
    kinetic,
    form_factor,
    sphere_index,
    atom_positions,
    proj_atom,
    coupling,
    potential,
):
    groups = lax.axis_size("fft")
    pools = lax.axis_size("kpool")
    bands = orbitals.shape[1]
    points = sphere_index.shape[1]
    columns = points // STICK_LEN
    slab = NG // groups
    atoms = atom_positions.shape[1]
    channels = form_factor.shape[2]
    share = atoms // groups
    cells = NG * NG
    count = groups * columns
    tile = 8 * NG
    scale = 2.0 / (pools * points * groups)
    line_high, line_low = line_matrix(columns, groups)

    index = sphere_index[0]
    own = index.reshape(columns, STICK_LEN)[:, 0:1] // NG
    lanes = jnp.arange(LANES, dtype=jnp.int32)[None, :]
    wound = ((own // NG * (lanes // NG) + own % NG * (lanes % NG)) % NG).astype(jnp.float32)
    theta = TWO_PI * (
        atom_positions[0][:, None] * signed(index // cells)[None, :]
        + atom_positions[1][:, None] * signed(index // NG % NG)[None, :]
        + atom_positions[2][:, None] * signed(index % NG)[None, :]
    )
    slots = proj_atom.reshape(channels, -1)
    held = lax.axis_index("fft") * share + lanes // (4 * bands)
    number = jnp.sum((slots[:, :, None] == held[None]).astype(jnp.float32), axis=1)
    herm_real = (0.5 * (coupling[0] + coupling[0].T)).reshape(2, channels, 2, channels)
    herm_imag = (0.5 * (coupling[1] - coupling[1].T)).reshape(2, channels, 2, channels)
    mixing = jnp.stack(
        [jnp.stack([herm_real, -herm_imag], 0), jnp.stack([herm_imag, herm_real], 0)], 0
    )
    mixing = jnp.transpose(mixing, (1, 4, 0, 2, 3, 5)).reshape(16 * channels, channels)
    per_band = jnp.broadcast_to(jnp.stack([old_norm[0], band_energy[0]])[:, :, None], (2, bands, LANES))

    def vmem(*shape):
        return pltpu.VMEM(shape, jnp.float32)

    def half(*shape):
        return pltpu.VMEM(shape, jnp.bfloat16)

    field = jax.ShapeDtypeStruct(orbitals.shape[1:], jnp.float32)
    out = pl.pallas_call(
        functools.partial(step_kernel, groups, pools, scale),
        out_shape=[field, field, field, jax.ShapeDtypeStruct(potential.shape, jnp.float32)],
        in_specs=[pl.BlockSpec(memory_space=pltpu.VMEM)] * 15,
        out_specs=[pl.BlockSpec(memory_space=pltpu.VMEM)] * 4,
        scratch_shapes=[
            vmem(2, 8, LANES),
            vmem(groups, 2, 8, LANES),
            vmem(groups, 2, columns, LANES),
            vmem(groups, 2, columns, LANES),
            vmem(groups, columns, LANES),
            vmem(groups, columns, LANES),
            vmem(groups, channels, LANES),
            vmem(groups, channels, LANES),
            vmem(groups, 2, columns, LANES),
            vmem(groups, 2, columns, LANES),
            vmem(channels, LANES),
            vmem(groups, channels, LANES),
            pltpu.SemaphoreType.DMA((6, groups)),
            pltpu.SemaphoreType.DMA((6, groups)),
            half(atoms * channels, 2 * points),
            half(atoms * channels, 2 * points),
            vmem(2, count, LANES),
            vmem(2, count, LANES),
            half(2 * count, 2 * tile),
            half(2 * count, 2 * tile),
            half(6 * bands * slab, 2 * count),
            half(6 * bands * slab, 2 * count),
            vmem(2 * count, 2 * bands * slab),
            vmem(bands, tile),
            vmem(4 * slab, bands, cells),
            vmem(4 * slab, cells),
            vmem(4 * slab, cells),
            pltpu.SemaphoreType.DMA((2,)),
            pltpu.SemaphoreType.DMA((2,)),
        ],
        compiler_params=pltpu.CompilerParams(
            collective_id=0, has_side_effects=True, vmem_limit_bytes=48 * 2**20
        ),
    )(
        orbitals[0], response[0], residual[0], old_direction[0], per_band, kinetic, form_factor[0],
        wound, jnp.cos(theta), jnp.sin(theta), number, mixing, potential,
        jnp.asarray(line_high), jnp.asarray(line_low),
    )
    density = out[3]
    if pools != 2:
        density = lax.psum(density, "kpool")
    return (out[0][None], out[1][None], out[2][None], density)


def solution(mesh):
    in_specs = (
        P("kpool", None, None, "fft"),
        P("kpool", None, None, "fft"),
        P("kpool", None, None, "fft"),
        P("kpool", None, None, "fft"),
        P("kpool", None),
        P("kpool", None),
        P("kpool", "fft"),
        P("kpool", None, None, "fft"),
        P("kpool", "fft"),
        P(),
        P(),
        P(),
        P(None, "fft", None),
    )
    out_specs = (
        P("kpool", None, None, "fft"),
        P("kpool", None, None, "fft"),
        P("kpool", None, None, "fft"),
        P(None, "fft", None),
    )
    return jax.shard_map(
        per_device, mesh=mesh, in_specs=in_specs, out_specs=out_specs, check_vma=False
    )
```

time: 97.3 us -> 56.4 us (0.58)
  Pallas kernels: 10.5 us -> 42.6 us
  waiting for transfers between devices: 19 us -> 0 us
  starting transfers between devices: 18 us -> 0 us
  local copies, waits for them, and re-layouts: 25.9 us -> 8.79 us
  other arithmetic: 14.1 us -> 3.57 us
  matrix products: 7.67 us -> 0 us
    pallas_call x1, Pallas kernels: 10.5 us -> 42.6 us  [per_device(): pl.pallas_call(functools.partial(step_kernel, groups, pools, scale), out_...]
    all_to_all x3 -> x0, waiting for transfers between devices: 16.6 us -> none  [exchange(): lax.all_to_all(values, 'fft', split_axis=0, concat_axis=0, tiled=True)]
    all_to_all x3 -> x0, starting transfers between devices: 16.4 us -> none  [exchange(): lax.all_to_all(values, 'fft', split_axis=0, concat_axis=0, tiled=True)]
    reshape x13 -> x0, local copies, waits for them, and re-layouts: 7.89 us -> none  [the longest x1 3.39 us: per_device(): jnp.transpose(values, (1, 4, 6, 5, 2, 0, 3)).reshape(slab * 6 * bands, -1)]
    dot_general x5 -> x0, matrix products: 7.67 us -> none  [the longest x1 2.56 us: per_device(): lax.dot_general(lines, fields.reshape(6 * bands, 2 * points), (((1,), (1,...]
    transpose x2 -> x0, local copies, waits for them, and re-layouts: 4.32 us -> none  [the longest x1 2.78 us: per_device(): jnp.transpose(values, (1, 4, 6, 5, 2, 0, 3)).reshape(slab * 6 * bands, -1)]
    unnamed x30 -> x25, local copies, waits for them, and re-layouts: 1.92 us -> 6.1 us
    all_to_all x3 -> x0, local copies, waits for them, and re-layouts: 3.82 us -> none  [exchange(): lax.all_to_all(values, 'fft', split_axis=0, concat_axis=0, tiled=True)]
  transfers between devices with their start and end apart: 4 -> 0, of which waited for: 4 -> 0; matrix products, arithmetic and copies ran while one was open for 14% -> 0% of each run, Pallas kernels for 0% -> 0%
where the time goes in v1:
time: 56.4 us; the launch traced here: 55.8 us
  Pallas kernels  42.6 us (76%)
  local copies, waits for them, and re-layouts  8.79 us (16%)
  other arithmetic  3.57 us (6%)
  between operations  0.79 us (1%)
    pallas_call x1, Pallas kernels, per_device(): pl.pallas_call(functools.partial(step_kernel, groups, pools, scale), out_...  42.6 us
    unnamed x25, local copies, waits for them, and re-layouts  6.1 us
    convert_element_type x2, other arithmetic, signed(): return jnp.where(values < NG // 2, values, values - NG).astype(jnp.float32)  1.36 us

profile of v1, /device:TPU:0, one launch (start us, length us, event | category | flops | bytes accessed | tf_op | source)
XLA Modules:
  0.0 55.8 jit_solution(9753962161166811527)
XLA Ops:
  0.6 0.0 copy-start
  0.7 0.8 %pad_maximum_fusion.1 = f32[2,8]{1,0:T(2,128)S(1)} fusion(f32[1,8]{1,0:T(1,128)} %param.20, f32[1,8]{1,0:T(1,128)} %param.19), kind=kLoop, calls=%fused_computation.47 | loop fusion | flops 16 | bytes 128 | tf_op jit(solution)/shard_map/stack | solution.py:429
  1.4 0.8 %slice_bitcast_fusion.3 = (f32[64]{0:T(128)S(1)}, f32[64]{0:T(128)S(1)}, f32[64]{0:T(128)S(1)}) fusion(f32[3,64]{1,0:T(4,128)} %param.24), kind=kLoop, calls=%fused_computation.58 | loop fusion | bytes 1536 | tf_op jit(solution)/shard_map/mul | solution.py:416
  2.2 0.5 broadcast.247
  2.7 1.3 %fusion.7 = (f32[1,256]{1,0:T(1,128)S(1)}, s32[256]{0:T(256)S(1)}, f32[1,256]{1,0:T(1,128)S(1)}, s32[1,256]{1,0:T(1,128)S(1)}) fusion(s32[1,256]{1,0:T(1,128)} %param.23, s32[]{:T(128)} %broadcast.247), kind=kLoop, calls=%fused_computation.44 | loop fusion | flops 11264 | bytes 5124 | tf_op jit(solution)/shard_map/convert_element_type | solution.py:36
  4.1 0.1 reshape_squeeze.3
  4.2 0.1 copy.35
  4.3 0.1 fusion.5.wound_ref
  4.4 0.1 broadcast_in_dim.8.bands_ref
  4.5 0.8 %eq.24 = s32[16,64]{1,0:T(8,128)S(1)} reshape(s32[1024]{0:T(1024)} %param.25) | data formatting | bytes 8192 | tf_op jit(solution)/shard_map/eq | solution.py:422
  5.2 0.2 convert_reduce_fusion.number_ref
  5.4 0.7 %slice_bitcast_fusion = (f32[32,32]{1,0:T(8,128)S(1)}, f32[1,32,32]{2,1,0:T(8,128)S(1)}) fusion(f32[2,32,32]{2,1,0:T(8,128)} %param.26), kind=kLoop, calls=%fused_computation.11 | loop fusion | bytes 16384 | tf_op jit(solution)/shard_map/squeeze | solution.py:424
  6.2 0.1 copy.30
  6.2 0.1 copy.36
  6.3 0.8 %fusion.3 = (f32[32,32]{1,0:T(8,128)S(1)}, f32[32,32]{1,0:T(8,128)S(1)}) fusion(f32[32,32]{0,1:T(8,128)S(1)} %copy.30, f32[2,32,32]{2,1,0:T(8,128)} %param.26, f32[1,32,32]{1,2,0:T(8,128)S(1)} %copy.36), kind=kLoop, calls=%fused_computation.10 | loop fusion | flops 4096 | bytes 24576 | tf_op jit(solution)/shard_map/mul | solution.py:424
  7.1 0.1 reshape.119
  7.2 0.1 stack_reshape.2
  7.3 0.0 copy-start.7
  7.4 0.3 fusion
  7.7 0.3 copy-done.7
  8.1 0.0 copy-done.3
  8.1 0.0 copy-done.4
  8.1 0.0 copy-done.5
  8.1 0.0 copy-done.6
  8.2 0.3 copy-done.8
  8.4 1.2 %copy-done.1 = bf16[1024,512]{1,0:T(8,128)(2,1)S(1)} copy-done((bf16[1024,512]{1,0:T(8,128)(2,1)S(1)}, bf16[1024,512]{1,0:T(8,128)(2,1)}, u32[]{:S(2)}) %copy-start.1) | copy-done | bytes 1048600
  9.6 0.9 %copy-done.2 = f32[4,4,4096]{2,1,0:T(4,128)S(1)} copy-done((f32[4,4,4096]{2,1,0:T(4,128)S(1)}, f32[4,4,4096]{2,1,0:T(4,128)}, u32[]{:S(2)}) %copy-start.2) | copy-done | bytes 262168
  10.6 42.6 %shard_map.174 = (f32[8,4,256]{2,1,0:T(4,128)S(1)}, f32[8,4,256]{2,1,0:T(4,128)S(1)}, f32[8,4,256]{2,1,0:T(4,128)S(1)}, f32[4,4,4096]{2,1,0:T(4,128)S(1)}) custom-call(f32[8,4,256]{2,1,0:T(4,128)S(1)} %bitcast.46, f32[8,4,256]{2,1,0:T(4,128)S(1)} %bitcast.47, f32[8,4,256]{2,1,0:T(4,128)S(1)} %bitcast.48, f32[8,4,256]{2,1,0:T(4,128)S(1)} %bitcast.49, ...), custom_call_target="tpu_custom_call" | custom-call | tf_op jit(solution)/shard_map/pallas_call | solution.py:438
  53.2 0.6 %copy.44 = f32[1,8,4,256]{3,2,1,0:T(4,128)} copy(f32[1,8,4,256]{3,2,1,0:T(4,128)S(1)} %bitcast.53) | data formatting | bytes 65536
  53.8 0.6 %copy.45 = f32[1,8,4,256]{3,2,1,0:T(4,128)} copy(f32[1,8,4,256]{3,2,1,0:T(4,128)S(1)} %bitcast.52) | data formatting | bytes 65536
  54.5 0.6 %copy.46 = f32[1,8,4,256]{3,2,1,0:T(4,128)} copy(f32[1,8,4,256]{3,2,1,0:T(4,128)S(1)} %bitcast.51) | data formatting | bytes 65536
  55.1 0.7 %copy.47 = f32[4,4,4096]{2,1,0:T(4,128)} copy(f32[4,4,4096]{2,1,0:T(4,128)S(1)} %get-tuple-element.42) | data formatting | bytes 524288
  (17 shorter events, 0.1 us)
Async XLA Ops:
  0.6 7.1 %copy-start = (bf16[1024,512]{1,0:T(8,128)(2,1)S(1)}, bf16[1024,512]{1,0:T(8,128)(2,1)}, u32[]{:S(2)}) copy-start(bf16[1024,512]{1,0:T(8,128)(2,1)} %constant.133.clone.line_low) | copy-start | bytes 3145732
  7.3 0.8 %copy-start.7 = (f32[1,2,16,256]{3,2,1,0:T(8,128)S(1)}, f32[1,2,16,256]{3,2,1,0:T(8,128)}, u32[]{:S(2)}) copy-start(f32[1,2,16,256]{3,2,1,0:T(8,128)} %param.22) | copy-start | bytes 98308
  7.3 0.8 %copy-start.3 = (f32[1,8,4,256]{3,2,1,0:T(4,128)S(1)}, f32[1,8,4,256]{3,2,1,0:T(4,128)}, u32[]{:S(2)}) copy-start(f32[1,8,4,256]{3,2,1,0:T(4,128)} %param.15) | copy-start | bytes 98308
  7.3 0.8 %copy-start.4 = (f32[1,8,4,256]{3,2,1,0:T(4,128)S(1)}, f32[1,8,4,256]{3,2,1,0:T(4,128)}, u32[]{:S(2)}) copy-start(f32[1,8,4,256]{3,2,1,0:T(4,128)} %param.16) | copy-start | bytes 98308
  7.4 0.8 %copy-start.5 = (f32[1,8,4,256]{3,2,1,0:T(4,128)S(1)}, f32[1,8,4,256]{3,2,1,0:T(4,128)}, u32[]{:S(2)}) copy-start(f32[1,8,4,256]{3,2,1,0:T(4,128)} %param.17) | copy-start | bytes 98308
  7.4 0.8 %copy-start.6 = (f32[1,8,4,256]{3,2,1,0:T(4,128)S(1)}, f32[1,8,4,256]{3,2,1,0:T(4,128)}, u32[]{:S(2)}) copy-start(f32[1,8,4,256]{3,2,1,0:T(4,128)} %param.18) | copy-start | bytes 98308
  7.7 0.7 %copy-start.8 = (f32[1,256]{1,0:T(1,128)S(1)}, f32[1,256]{1,0:T(1,128)}, u32[]{:S(2)}) copy-start(f32[1,256]{1,0:T(1,128)} %kinetic_ref.1) | copy-start | bytes 3076
  8.4 1.2 %copy-start.1 = (bf16[1024,512]{1,0:T(8,128)(2,1)S(1)}, bf16[1024,512]{1,0:T(8,128)(2,1)}, u32[]{:S(2)}) copy-start(bf16[1024,512]{1,0:T(8,128)(2,1)} %constant.132.clone.line_high) | copy-start | bytes 3145732
  9.6 0.9 %copy-start.2 = (f32[4,4,4096]{2,1,0:T(4,128)S(1)}, f32[4,4,4096]{2,1,0:T(4,128)}, u32[]{:S(2)}) copy-start(f32[4,4,4096]{2,1,0:T(4,128)} %potential_ref.1) | copy-start | bytes 786436

commit v2 on v1

--- a/solution.py
+++ b/solution.py
@@ -57,12 +57,13 @@
 
 def step_kernel(
     groups, pools, scale,
-    orbitals_ref, response_ref, residual_ref, previous_ref, bands_ref, kinetic_ref, form_ref,
-    wound_ref, cosine_ref, sine_ref, number_ref, mixing_ref, potential_ref, line_high, line_low,
+    orbitals_ref, response_ref, residual_ref, previous_ref, old_ref, energy_ref, kinetic_ref,
+    form_ref, index_ref, atoms_ref, slots_ref, coupling_ref, potential_far, line_far,
     next_response_ref, next_residual_ref, direction_ref, density_ref,
     first_out, first_in, ends_out, ends_in, lines_out, lines_in, amps_out, amps_in,
     back_out, back_in, share_out, share_in, send_sems, recv_sems,
-    tab_high, tab_low, carry, turn, high, low, values_high, values_low,
+    tab_high, tab_low, carry, turn, table, values,
+    cosine_ref, sine_ref, potential_ref, line_ref, near,
     sticks, curve, slope, pair_out, pair_in, pair_send, pair_recv,
 ):
     me = lax.axis_index("fft")
@@ -72,11 +73,11 @@
     slab = NG // groups
     cells = NG * NG
     channels = form_ref.shape[1]
-    atoms = cosine_ref.shape[0]
+    atoms = atoms_ref.shape[1]
     share = atoms // groups
     count = groups * columns
     block = 2 * bands
-    tile = high.shape[1] // 2
+    tile = table.shape[1] // 2
     steps = cells // tile
 
     def peer(k):
@@ -116,6 +117,10 @@
 
         each_peer(action)
 
+    line_copy = pltpu.make_async_copy(line_far, line_ref, near.at[0])
+    potential_copy = pltpu.make_async_copy(potential_far, potential_ref, near.at[1])
+    line_copy.start()
+    potential_copy.start()
     barrier = pltpu.get_barrier_semaphore()
     each_peer(
         lambda other: pl.semaphore_signal(
@@ -133,11 +138,41 @@
         norm = norm + residual_ref[:, part, :] * residual_ref[:, part, :]
     norm = jnp.sum(norm, axis=1, keepdims=True)
     first_out[0] = jnp.broadcast_to(norm, (bands, LANES))
-    first_out[1] = wound_ref[...]
+    digits = NG.bit_length() - 1
+    index = index_ref[...]
+    spot = lax.broadcasted_iota(jnp.int32, (columns, points), 1)
+    row = lax.broadcasted_iota(jnp.int32, (columns, points), 0) * STICK_LEN
+    heads = jnp.where(spot == row, jnp.broadcast_to(index, (columns, points)), 0)
+
+    def head(values):
+        return jnp.sum(values.astype(jnp.float32), axis=1, keepdims=True).astype(jnp.int32)
+
+    lane = lax.broadcasted_iota(jnp.int32, (columns, LANES), 1)
+    over, down = lane >> digits, lane & (NG - 1)
+    wound = head(heads >> (2 * digits)) * over + head((heads >> digits) & (NG - 1)) * down
+    first_out[1] = (wound & (NG - 1)).astype(jnp.float32)
+
+    def upright(values):
+        size = values.shape[1]
+        across = lax.broadcasted_iota(jnp.int32, (size, size), 1)
+        along = lax.broadcasted_iota(jnp.int32, (size, size), 0)
+        spread = jnp.where(across == along, jnp.broadcast_to(values, (size, size)), 0.0)
+        return jnp.sum(spread, axis=1, keepdims=True)
+
+    theta = jnp.zeros((atoms, points), jnp.float32)
+    for axis in range(3):
+        freq = signed((index >> ((2 - axis) * digits)) & (NG - 1))
+        theta = theta + upright(atoms_ref[axis : axis + 1, :]) * freq
+    theta = TWO_PI * theta
+    cosine_ref[...] = jnp.cos(theta)
+    sine_ref[...] = jnp.sin(theta)
+    old_norm = upright(old_ref[...])
+    energy = upright(energy_ref[...])
     pl.semaphore_wait(barrier, groups - 1 + (1 if pools == 2 else 0))
     send(FIRST, first_out, first_in, own=True)
 
-    lines = (line_high[...], line_low[...])
+    line_copy.wait()
+    lines = (line_ref[0], line_ref[1])
 
     def to_lines(rows):
         made = product(lines, split(jnp.concatenate(rows, axis=0)), ((1,), (1,)))
@@ -178,7 +213,7 @@
 
     arrive(FIRST, first_in)
     norm = jnp.sum(first_in[:, 0], axis=0)[:, 0:1]
-    ratio = norm / bands_ref[0, :, 0:1]
+    ratio = norm / old_norm
     direction = []
     for part in range(4):
         value = residual_ref[:, part, :] + ratio * previous_ref[:, part, :]
@@ -205,7 +240,7 @@
     carry[1] = jnp.sin(TWO_PI / NG * wound)
     turn[0] = jnp.cos(TWO_PI / NG * ahead)
     turn[1] = jnp.sin(TWO_PI / NG * ahead)
-    local = kinetic_ref[...] - bands_ref[1, :, 0:1]
+    local = kinetic_ref[...] - energy
     own_curve = jnp.zeros((bands, points), jnp.float32)
     for value in direction:
         own_curve = own_curve + local * value * value
@@ -221,24 +256,25 @@
         got = got.reshape(count, LANES).T
         got = jnp.concatenate([got[0:height], got[height : 2 * height]], axis=1)
         parts = split(got)
-        values_high[field * height : (field + 1) * height] = parts[0]
-        values_low[field * height : (field + 1) * height] = parts[1]
+        values[field * height : (field + 1) * height] = jnp.concatenate(
+            [parts[0], parts[0], parts[1]], axis=1
+        )
 
     def plane_step(index, _):
         place = pl.ds(pl.multiple_of(index * tile, tile), tile)
         for pair in range(tile // LANES):
             cosine, sine = carry[0], carry[1]
             left, right = pair * LANES, tile + pair * LANES
-            for out, c, s in zip((high, low), split(cosine), split(sine)):
-                out[0:count, left : left + LANES] = c
-                out[0:count, right : right + LANES] = s
-                out[count:, left : left + LANES] = -s
-                out[count:, right : right + LANES] = c
+            for k, c, s in zip((0, 1), split(cosine), split(sine)):
+                for base in (0, 4 * count) if k == 0 else (2 * count,):
+                    table[base : base + count, left : left + LANES] = c
+                    table[base : base + count, right : right + LANES] = s
+                    table[base + count : base + 2 * count, left : left + LANES] = -s
+                    table[base + count : base + 2 * count, right : right + LANES] = c
             carry[0] = cosine * turn[0] - sine * turn[1]
             carry[1] = sine * turn[0] + cosine * turn[1]
 
-        table = (high[...], low[...])
-        grid = product((values_high[...], values_low[...]), table, ((1,), (0,)))
+        grid = jnp.dot(values[...], table[...], preferred_element_type=jnp.float32)
         total = curve[...]
         fields = []
         for z in range(slab):
@@ -277,14 +313,35 @@
             fields.append(jnp.concatenate([new_pr, new_pi], axis=1))
             fields.append(jnp.concatenate([new_qr, new_qi], axis=1))
         curve[...] = total
-        sticks[...] += product(table, split(jnp.concatenate(fields, axis=0)), ((1,), (1,)))
+        pieces = (table[0 : 2 * count], table[2 * count : 4 * count])
+        sticks[...] += product(pieces, split(jnp.concatenate(fields, axis=0)), ((1,), (1,)))
         return 0
 
+    potential_copy.wait()
     lax.fori_loop(0, steps // 2, plane_step, 0)
 
     arrive(AMPS, amps_in)
-    summed = jnp.sum(amps_in[...], axis=0) * number_ref[...]
-    mixed_all = product(split(mixing_ref[...]), split(summed), ((1,), (0,)))
+    holder = lax.broadcasted_iota(jnp.int32, (channels, LANES), 1) // (4 * bands)
+    number = jnp.zeros((channels, LANES), jnp.float32)
+    for inner in range(share):
+        found = (slots_ref[...] == me * share + inner).astype(jnp.float32)
+        found = jnp.sum(found, axis=1, keepdims=True)
+        number = number + jnp.where(holder == inner, found, 0.0)
+    summed = jnp.sum(amps_in[...], axis=0) * number
+    herm_real = 0.5 * (coupling_ref[0] + coupling_ref[0].T)
+    herm_imag = 0.5 * (coupling_ref[1] - coupling_ref[1].T)
+    whole = ((herm_real, -herm_imag), (herm_imag, herm_real))
+    mixing = jnp.concatenate(
+        [
+            whole[u // 2][v // 2][
+                u % 2 * channels : (u % 2 + 1) * channels, v % 2 * channels : (v % 2 + 1) * channels
+            ]
+            for v in range(4)
+            for u in range(4)
+        ],
+        axis=0,
+    )
+    mixed_all = product(split(mixing), split(summed), ((1,), (0,)))
     spot = lax.broadcasted_iota(jnp.int32, (channels, LANES), 1) // bands % 4
     mixed = jnp.zeros((channels, LANES), jnp.float32)
     for v in range(4):
@@ -294,7 +351,7 @@
             if u != v:
                 moved = pltpu.roll(moved, bands * (u - v) % LANES, 1)
             mixed = mixed + jnp.where(spot == u, moved, 0.0)
-    share_out[0:channels] = mixed * number_ref[...]
+    share_out[0:channels] = mixed * number
     pairing = jnp.broadcast_to(jnp.sum(mixed * summed, axis=0, keepdims=True), (bands, LANES))
     lane = lax.broadcasted_iota(jnp.int32, (bands, LANES), 1) % bands
     row = lax.broadcasted_iota(jnp.int32, (bands, LANES), 0)
@@ -401,32 +458,11 @@
     slab = NG // groups
     atoms = atom_positions.shape[1]
     channels = form_factor.shape[2]
-    share = atoms // groups
     cells = NG * NG
     count = groups * columns
     tile = 8 * NG
     scale = 2.0 / (pools * points * groups)
-    line_high, line_low = line_matrix(columns, groups)
-
-    index = sphere_index[0]
-    own = index.reshape(columns, STICK_LEN)[:, 0:1] // NG
-    lanes = jnp.arange(LANES, dtype=jnp.int32)[None, :]
-    wound = ((own // NG * (lanes // NG) + own % NG * (lanes % NG)) % NG).astype(jnp.float32)
-    theta = TWO_PI * (
-        atom_positions[0][:, None] * signed(index // cells)[None, :]
-        + atom_positions[1][:, None] * signed(index // NG % NG)[None, :]
-        + atom_positions[2][:, None] * signed(index % NG)[None, :]
-    )
-    slots = proj_atom.reshape(channels, -1)
-    held = lax.axis_index("fft") * share + lanes // (4 * bands)
-    number = jnp.sum((slots[:, :, None] == held[None]).astype(jnp.float32), axis=1)
-    herm_real = (0.5 * (coupling[0] + coupling[0].T)).reshape(2, channels, 2, channels)
-    herm_imag = (0.5 * (coupling[1] - coupling[1].T)).reshape(2, channels, 2, channels)
-    mixing = jnp.stack(
-        [jnp.stack([herm_real, -herm_imag], 0), jnp.stack([herm_imag, herm_real], 0)], 0
-    )
-    mixing = jnp.transpose(mixing, (1, 4, 0, 2, 3, 5)).reshape(16 * channels, channels)
-    per_band = jnp.broadcast_to(jnp.stack([old_norm[0], band_energy[0]])[:, :, None], (2, bands, LANES))
+    lines = jnp.asarray(np.stack(line_matrix(columns, groups)))
 
     def vmem(*shape):
         return pltpu.VMEM(shape, jnp.float32)
@@ -438,7 +474,7 @@
     out = pl.pallas_call(
         functools.partial(step_kernel, groups, pools, scale),
         out_shape=[field, field, field, jax.ShapeDtypeStruct(potential.shape, jnp.float32)],
-        in_specs=[pl.BlockSpec(memory_space=pltpu.VMEM)] * 15,
+        in_specs=[pl.BlockSpec(memory_space=pltpu.VMEM)] * 12 + [pl.BlockSpec(memory_space=pltpu.HBM)] * 2,
         out_specs=[pl.BlockSpec(memory_space=pltpu.VMEM)] * 4,
         scratch_shapes=[
             vmem(2, 8, LANES),
@@ -459,10 +495,13 @@
             half(atoms * channels, 2 * points),
             vmem(2, count, LANES),
             vmem(2, count, LANES),
-            half(2 * count, 2 * tile),
-            half(2 * count, 2 * tile),
-            half(6 * bands * slab, 2 * count),
-            half(6 * bands * slab, 2 * count),
+            half(6 * count, 2 * tile),
+            half(6 * bands * slab, 6 * count),
+            vmem(atoms, points),
+            vmem(atoms, points),
+            vmem(*potential.shape),
+            half(*lines.shape),
+            pltpu.SemaphoreType.DMA((2,)),
             vmem(2 * count, 2 * bands * slab),
             vmem(bands, tile),
             vmem(4 * slab, bands, cells),
@@ -475,9 +514,9 @@
             collective_id=0, has_side_effects=True, vmem_limit_bytes=48 * 2**20
         ),
     )(
-        orbitals[0], response[0], residual[0], old_direction[0], per_band, kinetic, form_factor[0],
-        wound, jnp.cos(theta), jnp.sin(theta), number, mixing, potential,
-        jnp.asarray(line_high), jnp.asarray(line_low),
+        orbitals[0], response[0], residual[0], old_direction[0], old_norm, band_energy, kinetic,
+        form_factor[0], sphere_index, atom_positions, proj_atom.reshape(channels, -1), coupling,
+        potential, lines,
     )
     density = out[3]
     if pools != 2:

time: 56.4 us -> 58.5 us (1.037)
  local copies, waits for them, and re-layouts: 8.79 us -> 13.7 us
  other arithmetic: 3.57 us -> 0 us
  Pallas kernels: 42.6 us -> 43.4 us
    unnamed x25 -> x30, local copies, waits for them, and re-layouts: 6.1 us -> 13 us
    convert_element_type x3 -> x0, other arithmetic: 1.44 us -> none  [the longest x2 1.36 us: signed(): return jnp.where(values < NG // 2, values, values - NG).astype(jnp.float32)]
    squeeze x2 -> x0, local copies, waits for them, and re-layouts: 0.81 us -> none  [per_device(): coupling[1] - coupling[1].T]
    mul x1 -> x0, local copies, waits for them, and re-layouts: 0.8 us -> none  [per_device(): atom_positions[0][:, None] * signed(index // cells)[None, :]]
    pallas_call x1, Pallas kernels: 42.6 us -> 43.4 us  [per_device(): pl.pallas_call(functools.partial(step_kernel, groups, pools, scale), out_...]
    another operation x3 -> x0, other arithmetic: 0.79 us -> none  [the longest x1 0.77 us: per_device(): jnp.stack([old_norm[0], band_energy[0]])[:, :, None]]
    mul x3 -> x0, other arithmetic: 0.78 us -> none  [the longest x1 0.75 us: per_device(): 0.5 * (coupling[1] - coupling[1].T)]
    eq x1 -> x0, local copies, waits for them, and re-layouts: 0.76 us -> none  [per_device(): slots[:, :, None] == held[None]]
where the time goes in v2:
time: 58.5 us; the launch traced here: 57.8 us
  Pallas kernels  43.4 us (74%)
  local copies, waits for them, and re-layouts  13.7 us (23%)
  between operations  0.65 us (1%)
    pallas_call x1, Pallas kernels, per_device(): pl.pallas_call(functools.partial(step_kernel, groups, pools, scale), out_...  43.4 us
    unnamed x30, local copies, waits for them, and re-layouts  13 us

profile of v2, /device:TPU:0, one launch (start us, length us, event | category | flops | bytes accessed | tf_op | source)
XLA Modules:
  0.0 57.8 jit_solution(6179431481088500039)
XLA Ops:
  0.6 0.8 %reshape.11.slots_ref = s32[16,64]{1,0:T(8,128)S(1)} reshape(s32[1024]{0:T(1024)} %param.24) | data formatting | bytes 8192 | tf_op jit(solution)/shard_map/reshape | solution.py:518
  1.4 0.0 copy-start
  1.4 1.6 %copy-done = bf16[2,1024,512]{2,1,0:T(8,128)(2,1)S(1)} copy-done((bf16[2,1024,512]{2,1,0:T(8,128)(2,1)S(1)}, bf16[2,1024,512]{2,1,0:T(8,128)(2,1)}, u32[]{:S(2)}) %copy-start) | copy-done | bytes 2097176
  3.0 0.0 copy-start.1
  3.0 0.9 %copy-done.1 = f32[4,4,4096]{2,1,0:T(4,128)S(1)} copy-done((f32[4,4,4096]{2,1,0:T(4,128)S(1)}, f32[4,4,4096]{2,1,0:T(4,128)}, u32[]{:S(2)}) %copy-start.1) | copy-done | bytes 262168
  3.9 0.0 copy-start.2
  3.9 0.8 %copy-done.2 = f32[1,8,4,256]{3,2,1,0:T(4,128)S(1)} copy-done((f32[1,8,4,256]{3,2,1,0:T(4,128)S(1)}, f32[1,8,4,256]{3,2,1,0:T(4,128)}, u32[]{:S(2)}) %copy-start.2) | copy-done | bytes 32792
  4.7 0.0 copy-start.3
  4.7 0.8 %copy-done.3 = f32[1,8,4,256]{3,2,1,0:T(4,128)S(1)} copy-done((f32[1,8,4,256]{3,2,1,0:T(4,128)S(1)}, f32[1,8,4,256]{3,2,1,0:T(4,128)}, u32[]{:S(2)}) %copy-start.3) | copy-done | bytes 32792
  5.4 0.0 copy-start.4
  5.4 0.8 %copy-done.4 = f32[1,8,4,256]{3,2,1,0:T(4,128)S(1)} copy-done((f32[1,8,4,256]{3,2,1,0:T(4,128)S(1)}, f32[1,8,4,256]{3,2,1,0:T(4,128)}, u32[]{:S(2)}) %copy-start.4) | copy-done | bytes 32792
  6.2 0.0 copy-start.5
  6.2 0.8 %copy-done.5 = f32[1,8,4,256]{3,2,1,0:T(4,128)S(1)} copy-done((f32[1,8,4,256]{3,2,1,0:T(4,128)S(1)}, f32[1,8,4,256]{3,2,1,0:T(4,128)}, u32[]{:S(2)}) %copy-start.5) | copy-done | bytes 32792
  7.0 0.0 copy-start.6
  7.0 0.8 %copy-done.6 = f32[1,2,16,256]{3,2,1,0:T(8,128)S(1)} copy-done((f32[1,2,16,256]{3,2,1,0:T(8,128)S(1)}, f32[1,2,16,256]{3,2,1,0:T(8,128)}, u32[]{:S(2)}) %copy-start.6) | copy-done | bytes 32792
  7.7 0.0 copy-start.7
  7.7 0.8 %copy-done.7 = f32[2,32,32]{2,1,0:T(8,128)S(1)} copy-done((f32[2,32,32]{2,1,0:T(8,128)S(1)}, f32[2,32,32]{2,1,0:T(8,128)}, u32[]{:S(2)}) %copy-start.7) | copy-done | bytes 8216
  8.5 0.0 copy-start.8
  8.5 0.7 %copy-done.8 = f32[3,64]{1,0:T(4,128)S(1)} copy-done((f32[3,64]{1,0:T(4,128)S(1)}, f32[3,64]{1,0:T(4,128)}, u32[]{:S(2)}) %copy-start.8) | copy-done | bytes 792
  9.2 0.0 copy-start.9
  9.2 0.7 %copy-done.9 = f32[1,256]{1,0:T(1,128)S(1)} copy-done((f32[1,256]{1,0:T(1,128)S(1)}, f32[1,256]{1,0:T(1,128)}, u32[]{:S(2)}) %copy-start.9) | copy-done | bytes 1048
  9.8 0.0 copy-start.10
  9.8 0.7 %copy-done.10 = s32[1,256]{1,0:T(1,128)S(1)} copy-done((s32[1,256]{1,0:T(1,128)S(1)}, s32[1,256]{1,0:T(1,128)}, u32[]{:S(2)}) %copy-start.10) | copy-done | bytes 1048
  10.5 0.0 copy-start.11
  10.5 0.7 %copy-done.11 = f32[1,8]{1,0:T(1,128)S(1)} copy-done((f32[1,8]{1,0:T(1,128)S(1)}, f32[1,8]{1,0:T(1,128)}, u32[]{:S(2)}) %copy-start.11) | copy-done | bytes 56
  11.2 0.0 copy-start.12
  11.2 0.7 %copy-done.12 = f32[1,8]{1,0:T(1,128)S(1)} copy-done((f32[1,8]{1,0:T(1,128)S(1)}, f32[1,8]{1,0:T(1,128)}, u32[]{:S(2)}) %copy-start.12) | copy-done | bytes 56
  11.8 43.4 %shard_map.165 = (f32[8,4,256]{2,1,0:T(4,128)S(1)}, f32[8,4,256]{2,1,0:T(4,128)S(1)}, f32[8,4,256]{2,1,0:T(4,128)S(1)}, f32[4,4,4096]{2,1,0:T(4,128)S(1)}) custom-call(f32[8,4,256]{2,1,0:T(4,128)S(1)} %bitcast.8, f32[8,4,256]{2,1,0:T(4,128)S(1)} %bitcast.9, f32[8,4,256]{2,1,0:T(4,128)S(1)} %bitcast.10, f32[8,4,256]{2,1,0:T(4,128)S(1)} %bitcast.11, ...), custom_call_target="tpu_custom_call" | custom-call | tf_op jit(solution)/shard_map/pallas_call | solution.py:474
  55.3 0.6 %copy.22 = f32[1,8,4,256]{3,2,1,0:T(4,128)} copy(f32[1,8,4,256]{3,2,1,0:T(4,128)S(1)} %bitcast.15) | data formatting | bytes 65536
  55.9 0.6 %copy.23 = f32[1,8,4,256]{3,2,1,0:T(4,128)} copy(f32[1,8,4,256]{3,2,1,0:T(4,128)S(1)} %bitcast.14) | data formatting | bytes 65536
  56.5 0.6 %copy.24 = f32[1,8,4,256]{3,2,1,0:T(4,128)} copy(f32[1,8,4,256]{3,2,1,0:T(4,128)S(1)} %bitcast.13) | data formatting | bytes 65536
  57.1 0.7 %copy.25 = f32[4,4,4096]{2,1,0:T(4,128)} copy(f32[4,4,4096]{2,1,0:T(4,128)S(1)} %get-tuple-element.19) | data formatting | bytes 524288
Async XLA Ops:
  1.4 1.6 %copy-start = (bf16[2,1024,512]{2,1,0:T(8,128)(2,1)S(1)}, bf16[2,1024,512]{2,1,0:T(8,128)(2,1)}, u32[]{:S(2)}) copy-start(bf16[2,1024,512]{2,1,0:T(8,128)(2,1)} %constant.2.clone.line_far) | copy-start | bytes 6291460
  3.0 0.9 %copy-start.1 = (f32[4,4,4096]{2,1,0:T(4,128)S(1)}, f32[4,4,4096]{2,1,0:T(4,128)}, u32[]{:S(2)}) copy-start(f32[4,4,4096]{2,1,0:T(4,128)} %potential_far.1) | copy-start | bytes 786436
  3.9 0.8 %copy-start.2 = (f32[1,8,4,256]{3,2,1,0:T(4,128)S(1)}, f32[1,8,4,256]{3,2,1,0:T(4,128)}, u32[]{:S(2)}) copy-start(f32[1,8,4,256]{3,2,1,0:T(4,128)} %param.14) | copy-start | bytes 98308
  4.7 0.8 %copy-start.3 = (f32[1,8,4,256]{3,2,1,0:T(4,128)S(1)}, f32[1,8,4,256]{3,2,1,0:T(4,128)}, u32[]{:S(2)}) copy-start(f32[1,8,4,256]{3,2,1,0:T(4,128)} %param.15) | copy-start | bytes 98308
  5.4 0.8 %copy-start.4 = (f32[1,8,4,256]{3,2,1,0:T(4,128)S(1)}, f32[1,8,4,256]{3,2,1,0:T(4,128)}, u32[]{:S(2)}) copy-start(f32[1,8,4,256]{3,2,1,0:T(4,128)} %param.16) | copy-start | bytes 98308
  6.2 0.8 %copy-start.5 = (f32[1,8,4,256]{3,2,1,0:T(4,128)S(1)}, f32[1,8,4,256]{3,2,1,0:T(4,128)}, u32[]{:S(2)}) copy-start(f32[1,8,4,256]{3,2,1,0:T(4,128)} %param.17) | copy-start | bytes 98308
  7.0 0.8 %copy-start.6 = (f32[1,2,16,256]{3,2,1,0:T(8,128)S(1)}, f32[1,2,16,256]{3,2,1,0:T(8,128)}, u32[]{:S(2)}) copy-start(f32[1,2,16,256]{3,2,1,0:T(8,128)} %param.21) | copy-start | bytes 98308
  7.7 0.8 %copy-start.7 = (f32[2,32,32]{2,1,0:T(8,128)S(1)}, f32[2,32,32]{2,1,0:T(8,128)}, u32[]{:S(2)}) copy-start(f32[2,32,32]{2,1,0:T(8,128)} %coupling_ref.1) | copy-start | bytes 24580
  8.5 0.7 %copy-start.8 = (f32[3,64]{1,0:T(4,128)S(1)}, f32[3,64]{1,0:T(4,128)}, u32[]{:S(2)}) copy-start(f32[3,64]{1,0:T(4,128)} %atoms_ref.1) | copy-start | bytes 2308
  9.2 0.7 %copy-start.9 = (f32[1,256]{1,0:T(1,128)S(1)}, f32[1,256]{1,0:T(1,128)}, u32[]{:S(2)}) copy-start(f32[1,256]{1,0:T(1,128)} %kinetic_ref.1) | copy-start | bytes 3076
  9.8 0.7 %copy-start.10 = (s32[1,256]{1,0:T(1,128)S(1)}, s32[1,256]{1,0:T(1,128)}, u32[]{:S(2)}) copy-start(s32[1,256]{1,0:T(1,128)} %index_ref.1) | copy-start | bytes 3076
  10.5 0.7 %copy-start.11 = (f32[1,8]{1,0:T(1,128)S(1)}, f32[1,8]{1,0:T(1,128)}, u32[]{:S(2)}) copy-start(f32[1,8]{1,0:T(1,128)} %old_ref.1) | copy-start | bytes 100
  11.2 0.7 %copy-start.12 = (f32[1,8]{1,0:T(1,128)S(1)}, f32[1,8]{1,0:T(1,128)}, u32[]{:S(2)}) copy-start(f32[1,8]{1,0:T(1,128)} %energy_ref.1) | copy-start | bytes 100

commit v3 on v2

--- a/solution.py
+++ b/solution.py
@@ -433,6 +433,16 @@
         copy(SHARE, share_out, share_in, other).wait_send()
 
     each_peer(sent)
+
+
+def staged_kernel(groups, pools, scale, *refs):
+    far, rest, near, sems = refs[:12], refs[12:-13], refs[-13:-1], refs[-1]
+    copies = [pltpu.make_async_copy(a, b, sems.at[k]) for k, (a, b) in enumerate(zip(far, near))]
+    for one in copies:
+        one.start()
+    for one in copies:
+        one.wait()
+    step_kernel(groups, pools, scale, *near, *rest)
 
 
 def per_device(
@@ -470,11 +480,15 @@
     def half(*shape):
         return pltpu.VMEM(shape, jnp.bfloat16)
 
+    inputs = (
+        orbitals[0], response[0], residual[0], old_direction[0], old_norm, band_energy, kinetic,
+        form_factor[0], sphere_index, atom_positions, proj_atom.reshape(channels, -1), coupling,
+    )
     field = jax.ShapeDtypeStruct(orbitals.shape[1:], jnp.float32)
     out = pl.pallas_call(
-        functools.partial(step_kernel, groups, pools, scale),
+        functools.partial(staged_kernel, groups, pools, scale),
         out_shape=[field, field, field, jax.ShapeDtypeStruct(potential.shape, jnp.float32)],
-        in_specs=[pl.BlockSpec(memory_space=pltpu.VMEM)] * 12 + [pl.BlockSpec(memory_space=pltpu.HBM)] * 2,
+        in_specs=[pl.BlockSpec(memory_space=pltpu.HBM)] * 14,
         out_specs=[pl.BlockSpec(memory_space=pltpu.VMEM)] * 4,
         scratch_shapes=[
             vmem(2, 8, LANES),
@@ -509,15 +523,13 @@
             vmem(4 * slab, cells),
             pltpu.SemaphoreType.DMA((2,)),
             pltpu.SemaphoreType.DMA((2,)),
-        ],
+        ]
+        + [pltpu.VMEM(one.shape, one.dtype) for one in inputs]
+        + [pltpu.SemaphoreType.DMA((len(inputs),))],
         compiler_params=pltpu.CompilerParams(
             collective_id=0, has_side_effects=True, vmem_limit_bytes=48 * 2**20
         ),
-    )(
-        orbitals[0], response[0], residual[0], old_direction[0], old_norm, band_energy, kinetic,
-        form_factor[0], sphere_index, atom_positions, proj_atom.reshape(channels, -1), coupling,
-        potential, lines,
-    )
+    )(*inputs, potential, lines)
     density = out[3]
     if pools != 2:
         density = lax.psum(density, "kpool")

time: 58.5 us -> 58.9 us (level)
  no operation moved by 1% of the time
where the time goes in v3:
time: 58.9 us; the launch traced here: 58.2 us
  Pallas kernels  43.8 us (74%)
  local copies, waits for them, and re-layouts  13.7 us (23%)
  between operations  0.65 us (1%)
    pallas_call x1, Pallas kernels, per_device(): pl.pallas_call(functools.partial(staged_kernel, groups, pools, scale), ou...  43.8 us
    unnamed x30, local copies, waits for them, and re-layouts  13 us

profile of v3, /device:TPU:0, one launch (start us, length us, event | category | flops | bytes accessed | tf_op | source)
XLA Modules:
  0.0 58.2 jit_solution(13934959713533487235)
XLA Ops:
  0.6 0.8 %reshape.11.refs_10_ = s32[16,64]{1,0:T(8,128)S(1)} reshape(s32[1024]{0:T(1024)} %param.24) | data formatting | bytes 8192 | tf_op jit(solution)/shard_map/reshape | solution.py:485
  1.4 0.0 copy-start
  1.4 1.6 %copy-done = bf16[2,1024,512]{2,1,0:T(8,128)(2,1)S(1)} copy-done((bf16[2,1024,512]{2,1,0:T(8,128)(2,1)S(1)}, bf16[2,1024,512]{2,1,0:T(8,128)(2,1)}, u32[]{:S(2)}) %copy-start) | copy-done | bytes 2097176
  3.0 0.0 copy-start.1
  3.0 0.9 %copy-done.1 = f32[4,4,4096]{2,1,0:T(4,128)S(1)} copy-done((f32[4,4,4096]{2,1,0:T(4,128)S(1)}, f32[4,4,4096]{2,1,0:T(4,128)}, u32[]{:S(2)}) %copy-start.1) | copy-done | bytes 262168
  3.9 0.0 copy-start.2
  3.9 0.8 %copy-done.2 = f32[1,8,4,256]{3,2,1,0:T(4,128)S(1)} copy-done((f32[1,8,4,256]{3,2,1,0:T(4,128)S(1)}, f32[1,8,4,256]{3,2,1,0:T(4,128)}, u32[]{:S(2)}) %copy-start.2) | copy-done | bytes 32792
  4.7 0.0 copy-start.3
  4.7 0.8 %copy-done.3 = f32[1,8,4,256]{3,2,1,0:T(4,128)S(1)} copy-done((f32[1,8,4,256]{3,2,1,0:T(4,128)S(1)}, f32[1,8,4,256]{3,2,1,0:T(4,128)}, u32[]{:S(2)}) %copy-start.3) | copy-done | bytes 32792
  5.4 0.0 copy-start.4
  5.4 0.8 %copy-done.4 = f32[1,8,4,256]{3,2,1,0:T(4,128)S(1)} copy-done((f32[1,8,4,256]{3,2,1,0:T(4,128)S(1)}, f32[1,8,4,256]{3,2,1,0:T(4,128)}, u32[]{:S(2)}) %copy-start.4) | copy-done | bytes 32792
  6.2 0.0 copy-start.5
  6.2 0.8 %copy-done.5 = f32[1,8,4,256]{3,2,1,0:T(4,128)S(1)} copy-done((f32[1,8,4,256]{3,2,1,0:T(4,128)S(1)}, f32[1,8,4,256]{3,2,1,0:T(4,128)}, u32[]{:S(2)}) %copy-start.5) | copy-done | bytes 32792
  7.0 0.0 copy-start.6
  7.0 0.8 %copy-done.6 = f32[1,2,16,256]{3,2,1,0:T(8,128)S(1)} copy-done((f32[1,2,16,256]{3,2,1,0:T(8,128)S(1)}, f32[1,2,16,256]{3,2,1,0:T(8,128)}, u32[]{:S(2)}) %copy-start.6) | copy-done | bytes 32792
  7.7 0.0 copy-start.7
  7.7 0.8 %copy-done.7 = f32[2,32,32]{2,1,0:T(8,128)S(1)} copy-done((f32[2,32,32]{2,1,0:T(8,128)S(1)}, f32[2,32,32]{2,1,0:T(8,128)}, u32[]{:S(2)}) %copy-start.7) | copy-done | bytes 8216
  8.5 0.0 copy-start.8
  8.5 0.7 %copy-done.8 = f32[3,64]{1,0:T(4,128)S(1)} copy-done((f32[3,64]{1,0:T(4,128)S(1)}, f32[3,64]{1,0:T(4,128)}, u32[]{:S(2)}) %copy-start.8) | copy-done | bytes 792
  9.2 0.0 copy-start.9
  9.2 0.7 %copy-done.9 = f32[1,256]{1,0:T(1,128)S(1)} copy-done((f32[1,256]{1,0:T(1,128)S(1)}, f32[1,256]{1,0:T(1,128)}, u32[]{:S(2)}) %copy-start.9) | copy-done | bytes 1048
  9.8 0.0 copy-start.10
  9.8 0.7 %copy-done.10 = s32[1,256]{1,0:T(1,128)S(1)} copy-done((s32[1,256]{1,0:T(1,128)S(1)}, s32[1,256]{1,0:T(1,128)}, u32[]{:S(2)}) %copy-start.10) | copy-done | bytes 1048
  10.5 0.0 copy-start.11
  10.5 0.7 %copy-done.11 = f32[1,8]{1,0:T(1,128)S(1)} copy-done((f32[1,8]{1,0:T(1,128)S(1)}, f32[1,8]{1,0:T(1,128)}, u32[]{:S(2)}) %copy-start.11) | copy-done | bytes 56
  11.2 0.0 copy-start.12
  11.2 0.7 %copy-done.12 = f32[1,8]{1,0:T(1,128)S(1)} copy-done((f32[1,8]{1,0:T(1,128)S(1)}, f32[1,8]{1,0:T(1,128)}, u32[]{:S(2)}) %copy-start.12) | copy-done | bytes 56
  11.8 43.8 %shard_map.165 = (f32[8,4,256]{2,1,0:T(4,128)S(1)}, f32[8,4,256]{2,1,0:T(4,128)S(1)}, f32[8,4,256]{2,1,0:T(4,128)S(1)}, f32[4,4,4096]{2,1,0:T(4,128)S(1)}) custom-call(f32[8,4,256]{2,1,0:T(4,128)S(1)} %bitcast.8, f32[8,4,256]{2,1,0:T(4,128)S(1)} %bitcast.9, f32[8,4,256]{2,1,0:T(4,128)S(1)} %bitcast.10, f32[8,4,256]{2,1,0:T(4,128)S(1)} %bitcast.11, ...), custom_call_target="tpu_custom_call" | custom-call | tf_op jit(solution)/shard_map/pallas_call | solution.py:488
  55.6 0.6 %copy.22 = f32[1,8,4,256]{3,2,1,0:T(4,128)} copy(f32[1,8,4,256]{3,2,1,0:T(4,128)S(1)} %bitcast.15) | data formatting | bytes 65536
  56.2 0.6 %copy.23 = f32[1,8,4,256]{3,2,1,0:T(4,128)} copy(f32[1,8,4,256]{3,2,1,0:T(4,128)S(1)} %bitcast.14) | data formatting | bytes 65536
  56.9 0.6 %copy.24 = f32[1,8,4,256]{3,2,1,0:T(4,128)} copy(f32[1,8,4,256]{3,2,1,0:T(4,128)S(1)} %bitcast.13) | data formatting | bytes 65536
  57.5 0.7 %copy.25 = f32[4,4,4096]{2,1,0:T(4,128)} copy(f32[4,4,4096]{2,1,0:T(4,128)S(1)} %get-tuple-element.19) | data formatting | bytes 524288
Async XLA Ops:
  1.4 1.6 %copy-start = (bf16[2,1024,512]{2,1,0:T(8,128)(2,1)S(1)}, bf16[2,1024,512]{2,1,0:T(8,128)(2,1)}, u32[]{:S(2)}) copy-start(bf16[2,1024,512]{2,1,0:T(8,128)(2,1)} %constant.2.clone.refs_13_) | copy-start | bytes 6291460
  3.0 0.9 %copy-start.1 = (f32[4,4,4096]{2,1,0:T(4,128)S(1)}, f32[4,4,4096]{2,1,0:T(4,128)}, u32[]{:S(2)}) copy-start(f32[4,4,4096]{2,1,0:T(4,128)} %refs_12_.1) | copy-start | bytes 786436
  3.9 0.8 %copy-start.2 = (f32[1,8,4,256]{3,2,1,0:T(4,128)S(1)}, f32[1,8,4,256]{3,2,1,0:T(4,128)}, u32[]{:S(2)}) copy-start(f32[1,8,4,256]{3,2,1,0:T(4,128)} %param.14) | copy-start | bytes 98308
  4.7 0.8 %copy-start.3 = (f32[1,8,4,256]{3,2,1,0:T(4,128)S(1)}, f32[1,8,4,256]{3,2,1,0:T(4,128)}, u32[]{:S(2)}) copy-start(f32[1,8,4,256]{3,2,1,0:T(4,128)} %param.15) | copy-start | bytes 98308
  5.4 0.8 %copy-start.4 = (f32[1,8,4,256]{3,2,1,0:T(4,128)S(1)}, f32[1,8,4,256]{3,2,1,0:T(4,128)}, u32[]{:S(2)}) copy-start(f32[1,8,4,256]{3,2,1,0:T(4,128)} %param.16) | copy-start | bytes 98308
  6.2 0.8 %copy-start.5 = (f32[1,8,4,256]{3,2,1,0:T(4,128)S(1)}, f32[1,8,4,256]{3,2,1,0:T(4,128)}, u32[]{:S(2)}) copy-start(f32[1,8,4,256]{3,2,1,0:T(4,128)} %param.17) | copy-start | bytes 98308
  7.0 0.8 %copy-start.6 = (f32[1,2,16,256]{3,2,1,0:T(8,128)S(1)}, f32[1,2,16,256]{3,2,1,0:T(8,128)}, u32[]{:S(2)}) copy-start(f32[1,2,16,256]{3,2,1,0:T(8,128)} %param.21) | copy-start | bytes 98308
  7.7 0.8 %copy-start.7 = (f32[2,32,32]{2,1,0:T(8,128)S(1)}, f32[2,32,32]{2,1,0:T(8,128)}, u32[]{:S(2)}) copy-start(f32[2,32,32]{2,1,0:T(8,128)} %refs_11_.1) | copy-start | bytes 24580
  8.5 0.7 %copy-start.8 = (f32[3,64]{1,0:T(4,128)S(1)}, f32[3,64]{1,0:T(4,128)}, u32[]{:S(2)}) copy-start(f32[3,64]{1,0:T(4,128)} %refs_9_.1) | copy-start | bytes 2308
  9.2 0.7 %copy-start.9 = (f32[1,256]{1,0:T(1,128)S(1)}, f32[1,256]{1,0:T(1,128)}, u32[]{:S(2)}) copy-start(f32[1,256]{1,0:T(1,128)} %refs_6_.1) | copy-start | bytes 3076
  9.8 0.7 %copy-start.10 = (s32[1,256]{1,0:T(1,128)S(1)}, s32[1,256]{1,0:T(1,128)}, u32[]{:S(2)}) copy-start(s32[1,256]{1,0:T(1,128)} %refs_8_.1) | copy-start | bytes 3076
  10.5 0.7 %copy-start.11 = (f32[1,8]{1,0:T(1,128)S(1)}, f32[1,8]{1,0:T(1,128)}, u32[]{:S(2)}) copy-start(f32[1,8]{1,0:T(1,128)} %refs_4_.1) | copy-start | bytes 100
  11.2 0.7 %copy-start.12 = (f32[1,8]{1,0:T(1,128)S(1)}, f32[1,8]{1,0:T(1,128)}, u32[]{:S(2)}) copy-start(f32[1,8]{1,0:T(1,128)} %refs_5_.1) | copy-start | bytes 100
